TPU v7x, 32 devices: a whole 2x2x4 slice. The times are simulated.
32 devices in a mesh: dp: 4 (over y, x), fsdp: 8 (over z, core).
Axes of the slice: x: 2, y: 2, z: 4, core: 2. Of those that a mesh axis runs over, the one named last changes fastest.
Arguments:
- images: bfloat16 [512, 197, 384], P(('dp', 'fsdp')), may hold values from -6 to 6
- counts: int32 [32], P(('dp', 'fsdp')), may hold values from 15 to 16
- qkv_flat: bfloat16 [442368], P(('dp', 'fsdp')), may hold values from -0.3125 to 0.3125
- out_flat: bfloat16 [147456], P(('dp', 'fsdp')), may hold values from -1.25 to 1.25
- up_flat: bfloat16 [589824], P(('dp', 'fsdp')), may hold values from -0.3125 to 0.3125
- down_flat: bfloat16 [589824], P(('dp', 'fsdp')), may hold values from -0.15625 to 0.15625
- vectors: bfloat16 [4608], P(('dp', 'fsdp')), may hold values from -1.5 to 1.5, as said below
- cotangent: bfloat16 [512, 197, 384], P(('dp', 'fsdp')), may hold values from -6 to 6
Outputs:
- block_out: bfloat16 [512, 197, 384], P(('dp', 'fsdp'))
- input_grad: float32 [512, 197, 384], P(('dp', 'fsdp'))
- grad_qkv: float32 [442368], P(('dp', 'fsdp'))
- grad_out: float32 [147456], P(('dp', 'fsdp'))
- grad_up: float32 [589824], P(('dp', 'fsdp'))
- grad_down: float32 [589824], P(('dp', 'fsdp'))
- grad_vectors: float32 [4608], P(('dp', 'fsdp'))
Inputs may be any that keep to these rules, and one draw needn't show every extreme that they name: `counts`: slots at or past a device's count hold no image; their rows are ignored. `vectors`: the two norms' gains lie in 0.5 to 1.5.
All inputs are finite; a program needn't handle non-finite values.
Results may differ from a plain program's by a relative error of at most 0.009.
Values may be sent and summed in bfloat16 or wider, within the bound.
A program may use at most 192 MiB of HBM per device.

v0:
```python
import jax
import jax.numpy as jnp
from jax import lax
from jax.sharding import PartitionSpec as P

D = 384
HEADS = 6
HD = 64
FF = 1536


epsilon = 1e-06


def matmul(left, right):
    return jnp.dot(left, right, preferred_element_type=jnp.float32)


def layer_norm(rows, gain, shift):
    center = rows - jnp.mean(rows, axis=-1, keepdims=True)
    inverse = lax.rsqrt(jnp.mean(center * center, axis=-1, keepdims=True) + epsilon)
    normed = center * inverse
    return (normed * gain + shift, normed, inverse)


def norm_back(upstream, normed, inverse, gain):
    scaled = upstream * gain
    first_mean = jnp.mean(scaled, axis=-1, keepdims=True)
    second_mean = jnp.mean(scaled * normed, axis=-1, keepdims=True)
    return inverse * (scaled - first_mean - normed * second_mean)


def gelu_exact(values):
    return jax.nn.gelu(values, approximate=False)


def split_weights(gathered):
    qkv_weight = gathered[0].reshape(D, 3 * D)
    out_weight = gathered[1].reshape(D, D)
    up_weight = gathered[2].reshape(D, FF)
    down_weight = gathered[3].reshape(FF, D)
    flat_vectors = gathered[4].astype(jnp.float32)
    pieces = [flat_vectors[block_index * D : (block_index + 1) * D] for block_index in range(8)]
    return (qkv_weight, out_weight, up_weight, down_weight, pieces + [flat_vectors[8 * D :]])


def body(images, counts, qkv_flat, out_flat, up_flat, down_flat, vectors, cotangent):
    slot_count = images.shape[0]
    length = images.shape[1]
    tokens = slot_count * length
    score_scale = HD ** (-0.5)
    gathered = (
        lax.all_gather(qkv_flat, ("dp", "fsdp"), axis=0, tiled=True),
        lax.all_gather(out_flat, ("dp", "fsdp"), axis=0, tiled=True),
        lax.all_gather(up_flat, ("dp", "fsdp"), axis=0, tiled=True),
        lax.all_gather(down_flat, ("dp", "fsdp"), axis=0, tiled=True),
        lax.all_gather(vectors, ("dp", "fsdp"), axis=0, tiled=True),
    )
    qkv_weight, out_weight, up_weight, down_weight, pieces = split_weights(gathered)
    (
        gain_one,
        shift_one,
        gain_two,
        shift_two,
        query_bias,
        value_bias,
        out_bias,
        down_bias,
        up_bias,
    ) = pieces
    slot_valid = (jnp.arange(slot_count, dtype=jnp.int32) < counts[0]).astype(jnp.float32)
    row_valid = jnp.repeat(slot_valid, length)[:, None]
    inputs = images.astype(jnp.float32).reshape(tokens, D)
    normed_one_out, normed_one, inverse_one = layer_norm(inputs, gain_one, shift_one)
    attention_input = normed_one_out.astype(jnp.bfloat16)
    qkv_bias = jnp.concatenate([query_bias, jnp.zeros((D,), jnp.float32), value_bias])
    projected = (matmul(attention_input, qkv_weight) + qkv_bias).astype(jnp.bfloat16)
    projected = projected.reshape(slot_count, length, 3, HEADS, HD)
    query_rows = projected[:, :, 0]
    key_rows = projected[:, :, 1]
    value_rows = projected[:, :, 2]
    scores = (
        jnp.einsum("bqhd,bkhd->bhqk", query_rows, key_rows, preferred_element_type=jnp.float32)
        * score_scale
    )
    row_max = jnp.max(scores, axis=-1, keepdims=True)
    weights_exp = jnp.exp(scores - row_max)
    attention = weights_exp / jnp.sum(weights_exp, axis=-1, keepdims=True)
    attention_low = attention.astype(jnp.bfloat16)
    mixed = jnp.einsum(
        "bhqk,bkhd->bqhd", attention_low, value_rows, preferred_element_type=jnp.float32
    )
    mixed_low = mixed.astype(jnp.bfloat16).reshape(tokens, D)
    residual = inputs + matmul(mixed_low, out_weight) + out_bias
    normed_two_out, normed_two, inverse_two = layer_norm(residual, gain_two, shift_two)
    hidden_input = normed_two_out.astype(jnp.bfloat16)
    up_sum = matmul(hidden_input, up_weight) + up_bias
    activated, gelu_pull = jax.vjp(gelu_exact, up_sum)
    activated_low = activated.astype(jnp.bfloat16)
    block_sum = residual + matmul(activated_low, down_weight) + down_bias
    block_out = (block_sum * row_valid).astype(jnp.bfloat16).reshape(slot_count, length, D)
    regathered = (
        lax.all_gather(qkv_flat, ("dp", "fsdp"), axis=0, tiled=True),
        lax.all_gather(out_flat, ("dp", "fsdp"), axis=0, tiled=True),
        lax.all_gather(up_flat, ("dp", "fsdp"), axis=0, tiled=True),
        lax.all_gather(down_flat, ("dp", "fsdp"), axis=0, tiled=True),
        lax.all_gather(vectors, ("dp", "fsdp"), axis=0, tiled=True),
    )
    qkv_weight, out_weight, up_weight, down_weight, pieces = split_weights(regathered)
    gain_one = pieces[0]
    gain_two = pieces[2]
    upstream = cotangent.astype(jnp.float32).reshape(tokens, D) * row_valid
    upstream_low = upstream.astype(jnp.bfloat16)
    grad_down = matmul(activated_low.T, upstream_low)
    grad_down_bias = jnp.sum(upstream_low.astype(jnp.float32), axis=0)
    (grad_up_sum,) = gelu_pull(matmul(upstream_low, down_weight.T))
    up_low = grad_up_sum.astype(jnp.bfloat16)
    grad_up = matmul(hidden_input.T, up_low)
    grad_up_bias = jnp.sum(up_low.astype(jnp.float32), axis=0)
    back_two = matmul(up_low, up_weight.T)
    grad_gain_two = jnp.sum(back_two * normed_two, axis=0)
    grad_shift_two = jnp.sum(back_two, axis=0)
    grad_residual = upstream + norm_back(back_two, normed_two, inverse_two, gain_two)
    residual_low = grad_residual.astype(jnp.bfloat16)
    grad_out = matmul(mixed_low.T, residual_low)
    grad_out_bias = jnp.sum(residual_low.astype(jnp.float32), axis=0)
    mixed_grad = (
        matmul(residual_low, out_weight.T)
        .astype(jnp.bfloat16)
        .reshape(slot_count, length, HEADS, HD)
    )
    value_grad = jnp.einsum(
        "bhqk,bqhd->bkhd", attention_low, mixed_grad, preferred_element_type=jnp.float32
    )
    weight_grad = jnp.einsum(
        "bqhd,bkhd->bhqk", mixed_grad, value_rows, preferred_element_type=jnp.float32
    )
    row_dot = jnp.sum(weight_grad * attention, axis=-1, keepdims=True)
    score_grad = (attention * (weight_grad - row_dot)).astype(jnp.bfloat16)
    query_grad = (
        jnp.einsum("bhqk,bkhd->bqhd", score_grad, key_rows, preferred_element_type=jnp.float32)
        * score_scale
    )
    key_grad = (
        jnp.einsum("bhqk,bqhd->bkhd", score_grad, query_rows, preferred_element_type=jnp.float32)
        * score_scale
    )
    projected_grad = (
        jnp.stack([query_grad, key_grad, value_grad], axis=2)
        .reshape(tokens, 3 * D)
        .astype(jnp.bfloat16)
    )
    grad_qkv = matmul(attention_input.T, projected_grad)
    bias_sums = jnp.sum(projected_grad.astype(jnp.float32), axis=0)
    back_one = matmul(projected_grad, qkv_weight.T)
    grad_gain_one = jnp.sum(back_one * normed_one, axis=0)
    grad_shift_one = jnp.sum(back_one, axis=0)
    input_grad = grad_residual + norm_back(back_one, normed_one, inverse_one, gain_one)
    grad_vectors = jnp.concatenate(
        [
            grad_gain_one,
            grad_shift_one,
            grad_gain_two,
            grad_shift_two,
            bias_sums[:D],
            bias_sums[2 * D :],
            grad_out_bias,
            grad_down_bias,
            grad_up_bias,
        ]
    )
    qkv_shard, out_shard, up_shard, down_shard, vector_shard = (
        lax.psum_scatter(grad_qkv.reshape(-1), ("dp", "fsdp"), scatter_dimension=0, tiled=True),
        lax.psum_scatter(grad_out.reshape(-1), ("dp", "fsdp"), scatter_dimension=0, tiled=True),
        lax.psum_scatter(grad_up.reshape(-1), ("dp", "fsdp"), scatter_dimension=0, tiled=True),
        lax.psum_scatter(grad_down.reshape(-1), ("dp", "fsdp"), scatter_dimension=0, tiled=True),
        lax.psum_scatter(grad_vectors, ("dp", "fsdp"), scatter_dimension=0, tiled=True),
    )
    return (
        block_out,
        input_grad.reshape(slot_count, length, D),
        qkv_shard,
        out_shard,
        up_shard,
        down_shard,
        vector_shard,
    )


def solution(mesh):
    return jax.shard_map(
        body,
        mesh=mesh,
        in_specs=(
            P(("dp", "fsdp"), None, None),
            P(("dp", "fsdp")),
            P(("dp", "fsdp")),
            P(("dp", "fsdp")),
            P(("dp", "fsdp")),
            P(("dp", "fsdp")),
            P(("dp", "fsdp")),
            P(("dp", "fsdp"), None, None),
        ),
        out_specs=(
            P(("dp", "fsdp"), None, None),
            P(("dp", "fsdp"), None, None),
            P(("dp", "fsdp")),
            P(("dp", "fsdp")),
            P(("dp", "fsdp")),
            P(("dp", "fsdp")),
            P(("dp", "fsdp")),
        ),
        check_vma=False,
    )
```

profile of v0, /device:TPU:0, one launch (start us, length us, event | category | flops | bytes accessed | tf_op | source)
XLA Modules:
  0.0 748.1 jit_solution(14363793167931195562)
XLA Ops:
  15.6 42.2 %all-reduce = bf16[4608]{0:T(1024)(128)(2,1)S(1)} all-reduce(bf16[4608]{0:T(1024)(128)(2,1)S(1)} %dynamic-update-slice), channel_id=1, replica_groups=mesh['dp'=4,'fsdp'=8] {'dp','fsdp'}, use_global_device_ids=true, to_apply=%add | all-reduce | flops 4608 | bytes 18432
  65.6 51.2 %all-gather = bf16[32,1,13824]{2,1,0:T(2,128)(2,1)S(1)} all-gather(bf16[1,1,13824]{2,1,0:T(2,128)(2,1)S(1)} %reshape.218), channel_id=1, replica_groups=mesh['dp'=4,'fsdp'=8] {'dp','fsdp'}, dimensions={0}, use_global_device_ids=true | all-gather | bytes 912384 | tf_op jit(solution)/shard_map/all_gather | solution.py:53
  123.5 9.2 %fusion.8 = bf16[3152,1152]{1,0:T(8,128)(2,1)} fusion(bf16[3152,384]{1,0:T(8,128)(2,1)} %convert_element_type.94, bf16[384,1152]{1,0:T(8,128)(2,1)S(1)} %reshape.202, f32[1152]{0:T(1024)S(1)} %pad_maximum_fusion.1), kind=kOutput, calls=%fused_computation.26 | convolution fusion | flops 2795950080 | bytes 10572288 | tf_op jit(solution)/shard_map/dot_general | solution.py:16
  132.7 22.3 %reshape.224 = bf16[16,197,3,6,64]{4,3,2,1,0:T(8,128)(2,1)} reshape(bf16[3152,1152]{1,0:T(8,128)(2,1)} %fusion.8) | data formatting | bytes 14524416 | tf_op jit(solution)/shard_map/reshape | solution.py:78
  155.1 15.3 %fusion.51 = (bf16[16,197,1,6,64]{4,3,2,1,0:T(8,128)(2,1)}, bf16[16,197,1,6,64]{4,3,2,1,0:T(8,128)(2,1)}, bf16[16,197,1,6,64]{4,3,2,1,0:T(8,128)(2,1)}) fusion(bf16[16,197,3,6,64]{4,3,2,1,0:T(8,128)(2,1)} %reshape.224), kind=kLoop, calls=%fused_computation.103 | loop fusion | bytes 14524416 | tf_op jit(solution)/shard_map/slice | solution.py:79
  185.0 12.5 %fusion.24 = f32[16,6,197,197]{2,3,1,0:T(8,128)} fusion(bf16[16,197,1,6,64]{1,4,3,0,2:T(8,128)(2,1)S(1)} %copy.103, bf16[16,197,1,6,64]{1,4,3,0,2:T(8,128)(2,1)} %copy.102), kind=kOutput, calls=%fused_computation.66 | convolution fusion | flops 476884992 | bytes 19744128 | tf_op jit(solution)/shard_map/bqhd,bkhd->bhqk/dot_general | solution.py:83
  197.5 22.3 %fusion.54 = (f32[16,6,197]{2,1,0:T(8,128)S(1)}, f32[16,6,197,197]{2,3,1,0:T(8,128)}) fusion(f32[16,6,197,197]{2,3,1,0:T(8,128)} %fusion.24), kind=kOutput, calls=%fused_computation.106 | output fusion | flops 14902852 | bytes 29880960 | tf_op jit(solution)/shard_map/sub | solution.py:87
  226.6 9.8 %convert_bitcast_fusion.1 = bf16[16,197,6,64]{1,3,2,0:T(8,128)(2,1)S(1)} fusion(bf16[16,197,1,6,64]{1,4,3,0,2:T(8,128)(2,1)S(1)} %copy.101, f32[16,6,197,197]{2,3,1,0:T(8,128)} %get-tuple-element.69, f32[16,6,197]{2,1,0:T(8,128)S(1)} %get-tuple-element.68), kind=kOutput, calls=%fused_computation.75 | convolution fusion | flops 485546688 | bytes 19819776 | tf_op jit(solution)/shard_map/bhqk,bkhd->bqhd/dot_general | solution.py:90
  251.1 39.1 %all-gather.1 = bf16[32,1,4608]{2,1,0:T(2,128)(2,1)S(1)} all-gather(bf16[1,1,4608]{2,1,0:T(2,128)(2,1)S(1)} %reshape.220), channel_id=1, replica_groups=mesh['dp'=4,'fsdp'=8] {'dp','fsdp'}, dimensions={0}, use_global_device_ids=true | all-gather | bytes 304128 | tf_op jit(solution)/shard_map/all_gather | solution.py:54
  315.7 50.9 %multiply_convert_fusion.1 = (bf16[3152,1536]{1,0:T(8,128)(2,1)}, f32[3152,1536]{1,0:T(8,128)}, f32[3152,1536]{1,0:T(8,128)}) fusion(f32[1536]{0:T(1024)S(1)} %slice.76, bf16[384,1536]{1,0:T(8,128)(2,1)} %reshape.206, f32[3152,384]{1,0:T(8,128)} %copy-done.2, f32[384]{0:T(512)S(1)} %get-tuple-element.62, f32[384]{0:T(512)S(1)} %get-tuple-element.61, ...), kind=kOutput, calls=%fused_computation.9 | convolution fusion | flops 4043839488 | bytes 54470272 | tf_op jit(solution)/shard_map/dot_general | solution.py:16
  369.7 22.3 %convert_reduce_fusion = (f32[1536]{0:T(1024)}, bf16[3152,1536]{1,0:T(8,128)(2,1)}) fusion(f32[3152,1536]{1,0:T(8,128)} %get-tuple-element.54, bf16[3152,384]{1,0:T(8,128)(2,1)S(1)} %copy-done.18, bf16[1536,384]{1,0:T(8,128)(2,1)} %reshape.207, f32[3152,1536]{1,0:T(8,128)} %get-tuple-element.72, f32[1536]{0:T(1024)S(1)} %slice.76), kind=kOutput, calls=%fused_computation.7 | convolution fusion | flops 3800553984 | bytes 52027392 | tf_op jit(solution)/shard_map/dot_general | solution.py:16
  392.1 11.5 %multiply_reduce_fusion.2 = (f32[384]{0:T(512)}, f32[3152]{0:T(1024)S(1)}, f32[3152]{0:T(1024)S(1)}, f32[384]{0:T(512)}, f32[3152,384]{1,0:T(8,128)S(1)}) fusion(f32[3152,384]{1,0:T(8,128)S(1)} %bitcast.72, f32[3152]{0:T(1024)S(1)} %add_rsqrt_fusion, f32[3152]{0:T(1024)S(1)} %broadcast_multiply_fusion.4, f32[384]{0:T(512)S(1)} %get-tuple-element.61, ...), kind=kOutput, calls=%fused_computation.45 | convolution fusion | flops 3729136640 | bytes 20600576 | tf_op jit(solution)/shard_map/dot_general | solution.py:16
  424.8 14.2 %multiply_reduce_fusion = (f32[16,6,197]{2,1,0:T(8,128)S(1)}, f32[16,6,197,197]{2,3,1,0:T(8,128)}) fusion(f32[16,6,197,197]{2,3,1,0:T(8,128)} %get-tuple-element.69, f32[16,6,197]{2,1,0:T(8,128)S(1)} %copy-done.25, bf16[16,197,6,64]{1,3,2,0:T(8,128)(2,1)} %copy.85, bf16[16,197,1,6,64]{1,4,3,0,2:T(8,128)(2,1)S(1)} %copy-done.14), kind=kOutput, calls=%fused_computation.3 | convolution fusion | flops 488043072 | bytes 34798080 | tf_op jit(solution)/shard_map/bqhd,bkhd->bhqk/dot_general | solution.py:135
  439.0 14.3 %multiply_convert_fusion = bf16[16,6,197,197]{2,3,1,0:T(8,128)(2,1)S(1)} fusion(f32[16,6,197,197]{2,3,1,0:T(8,128)} %get-tuple-element.75, f32[16,6,197]{2,1,0:T(8,128)S(1)} %get-tuple-element.74, f32[16,6,197,197]{2,3,1,0:T(8,128)} %get-tuple-element.69, f32[16,6,197]{2,1,0:T(8,128)S(1)} %copy-done.25), kind=kLoop, calls=%fused_computation.2 | loop fusion | flops 14902656 | bytes 37407936 | tf_op jit(solution)/shard_map/convert_element_type | solution.py:139
  460.6 8.8 %fusion.21 = bf16[16,197,1,6,64]{1,4,3,0,2:T(8,128)(2,1)} fusion(bf16[16,6,197,197]{2,3,1,0:T(8,128)(2,1)} %copy-done, bf16[16,197,1,6,64]{1,4,3,0,2:T(8,128)(2,1)S(1)} %copy-done.8), kind=kOutput, calls=%fused_computation.63 | convolution fusion | flops 479305728 | bytes 12292800 | tf_op jit(solution)/shard_map/bhqk,bqhd->bkhd/dot_general | solution.py:145
  469.3 10.8 %convert_bitcast_fusion = bf16[16,197,1,6,64]{1,4,3,0,2:T(8,128)(2,1)S(1)} fusion(bf16[16,197,6,64]{1,3,2,0:T(8,128)(2,1)} %copy.85, f32[16,6,197,197]{2,3,1,0:T(8,128)} %get-tuple-element.69, f32[16,6,197]{2,1,0:T(8,128)S(1)} %copy-done.25), kind=kOutput, calls=%fused_computation.74 | convolution fusion | flops 485546688 | bytes 19819776 | tf_op jit(solution)/shard_map/bhqk,bqhd->bkhd/dot_general | solution.py:132
  480.1 11.1 %fusion.48 = f32[384,1536]{1,0:T(8,128)} fusion(bf16[3152,1536]{1,0:T(8,128)(2,1)} %get-tuple-element.78, f32[3152,384]{1,0:T(8,128)} %copy-done.2, f32[384]{0:T(512)S(1)} %get-tuple-element.62, f32[384]{0:T(512)S(1)} %get-tuple-element.61, f32[3152]{0:T(1024)S(1)} %add_rsqrt_fusion, f32[3152]{0:T(1024)S(1)} %broadcast_multiply_fusion.4), kind=kOutput, calls=%fused_computation.101 | convolution fusion | flops 3724302336 | bytes 16912000 | tf_op jit(solution)/shard_map/dot_general | solution.py:16
  501.1 13.9 %copy.90 = bf16[16,197,3,6,64]{1,0,4,3,2:T(8,128)(2,1)} copy(bf16[16,197,3,6,64]{1,4,3,0,2:T(8,128)(2,1)} %get-tuple-element.52) | data formatting | bytes 14524416 | tf_op jit(solution)/shard_map/stack | solution.py:149
  515.0 18.7 %convert_element_type.110 = bf16[3152,1152]{0,1:T(8,128)(2,1)} reshape(bf16[16,197,3,6,64]{1,0,4,3,2:T(8,128)(2,1)} %copy.90) | data formatting | bytes 14524416 | tf_op jit(solution)/shard_map/convert_element_type | solution.py:151
  548.5 9.9 %fusion.32 = f32[1536,384]{1,0:T(8,128)S(1)} fusion(bf16[3152,1536]{1,0:T(8,128)(2,1)} %get-tuple-element.53, f32[3152,384]{1,0:T(8,128)} %reshape.209, f32[3152]{0:T(1024)S(1)} %copy-done.28), kind=kOutput, calls=%fused_computation.76 | convolution fusion | flops 3720671232 | bytes 16896320 | tf_op jit(solution)/shard_map/dot_general | solution.py:16
  560.0 12.0 %multiply_reduce_fusion.3 = (f32[384]{0:T(512)S(1)}, f32[3152]{0:T(1024)S(1)}, f32[3152]{0:T(1024)S(1)}, f32[384]{0:T(512)S(1)}, f32[3152,384]{1,0:T(8,128)}) fusion(f32[3152,384]{1,0:T(8,128)} %reshape.201, f32[3152]{0:T(1024)S(1)} %copy-done.27, f32[3152]{0:T(1024)S(1)} %copy-done.26, f32[384]{0:T(512)S(1)} %copy-done.32, ...), kind=kOutput, calls=%fused_computation.46 | convolution fusion | flops 2799574016 | bytes 17884928 | tf_op jit(solution)/shard_map/dot_general | solution.py:16
  590.8 9.5 %fusion.15 = bf16[3152,384]{1,0:T(8,128)(2,1)} fusion(f32[3152,384]{1,0:T(8,128)S(1)} %bitcast.74, bf16[3152,1536]{1,0:T(8,128)(2,1)} %get-tuple-element.53, bf16[1536,384]{1,0:T(8,128)(2,1)S(1)} %copy-done.20, f32[3152]{0:T(1024)S(1)} %copy-done.28, f32[384]{0:T(512)S(1)} %copy-done.37), kind=kOutput, calls=%fused_computation.38 | convolution fusion | flops 3723091968 | bytes 18138944 | tf_op jit(solution)/shard_map/dot_general | solution.py:16
  604.3 40.1 %all-reduce.5 = f32[4608]{0:T(1024)S(1)} all-reduce(f32[4608]{0:T(1024)S(1)} %constant_dynamic-update-slice_fusion), channel_id=6, replica_groups=mesh['dp'=4,'fsdp'=8] {'dp','fsdp'}, use_global_device_ids=true, to_apply=%region_23.0.clone | all-reduce | flops 4608 | bytes 36864
  645.1 90.1 %all-reduce.9.cloned.1.call-done = (f32[442368]{0:T(1024)}, f32[147456]{0:T(1024)}, f32[589824]{0:T(1024)}, f32[589824]{0:T(1024)}) async-done(((f32[442368]{0:T(1024)}, f32[147456]{0:T(1024)}, f32[589824]{0:T(1024)}, f32[589824]{0:T(1024)}), (f32[442368]{0:T(1024)}, f32[147456]{0:T(1024)}, f32[589824]{0:T(1024)}, f32[589824]{0:T(1024)})) %all-reduce.9.cloned.1.call-update) | async-done | bytes 7077904
  (184 shorter events, 169.3 us)
Async XLA Ops:
  7.2 305.0 %all-gather.5.cloned.1.call-start = ((), (), s32[]{:S(2)}) async-start(), calls=%async_computation | async-start | bytes 1216512 | tf_op jit(solution)/shard_map/all_gather | solution.py:55
  7.9 358.7 %all-gather.7.cloned.1.call-start = ((), (), s32[]{:S(2)}) async-start(), calls=%async_computation.1 | async-start | bytes 1216512 | tf_op jit(solution)/shard_map/all_gather | solution.py:56
  8.6 726.5 %all-reduce.9.cloned.1.call-start = ((), (), s32[]{:S(2)}) async-start(), calls=%async_computation.2 | async-start | bytes 14155776
  8.7 49.9 %copy-start.5 = (bf16[16,197,384]{2,0,1:T(8,128)(2,1)S(1)}, bf16[16,197,384]{2,0,1:T(8,128)(2,1)}, u32[]{:S(2)}) copy-start(bf16[16,197,384]{2,0,1:T(8,128)(2,1)} %param.8) | copy-start | bytes 7262212
  123.5 9.2 %copy-start.22 = (bf16[384,1152]{1,0:T(8,128)(2,1)}, bf16[384,1152]{1,0:T(8,128)(2,1)S(1)}, u32[]{:S(2)}) copy-start(bf16[384,1152]{1,0:T(8,128)(2,1)S(1)} %reshape.202) | copy-start | bytes 2654212
  185.0 12.5 %copy-start.3 = (bf16[16,197,1,6,64]{1,4,3,0,2:T(8,128)(2,1)}, bf16[16,197,1,6,64]{1,4,3,0,2:T(8,128)(2,1)S(1)}, u32[]{:S(2)}) copy-start(bf16[16,197,1,6,64]{1,4,3,0,2:T(8,128)(2,1)S(1)} %copy.103) | copy-start | bytes 7262212
  219.8 16.6 %copy-start.24 = (f32[16,6,197]{2,1,0:T(8,128)}, f32[16,6,197]{2,1,0:T(8,128)S(1)}, u32[]{:S(2)}) copy-start(f32[16,6,197]{2,1,0:T(8,128)S(1)} %get-tuple-element.68) | copy-start | bytes 226948
  226.6 9.8 %copy-start.13 = (bf16[16,197,1,6,64]{1,4,3,0,2:T(8,128)(2,1)}, bf16[16,197,1,6,64]{1,4,3,0,2:T(8,128)(2,1)S(1)}, u32[]{:S(2)}) copy-start(bf16[16,197,1,6,64]{1,4,3,0,2:T(8,128)(2,1)S(1)} %copy.101) | copy-start | bytes 7262212
  246.0 46.3 %copy-start.6 = (bf16[3152,384]{0,1:T(8,128)(2,1)}, bf16[3152,384]{0,1:T(8,128)(2,1)S(1)}, u32[]{:S(2)}) copy-start(bf16[3152,384]{0,1:T(8,128)(2,1)S(1)} %reshape.204) | copy-start | bytes 7262212
  315.7 54.0 %copy-start.18 = (bf16[3152,384]{1,0:T(8,128)(2,1)S(1)}, bf16[3152,384]{1,0:T(8,128)(2,1)}, u32[]{:S(2)}) copy-start(bf16[3152,384]{1,0:T(8,128)(2,1)} %convert_element_type.105) | copy-start | bytes 7262212
  366.6 25.5 %slice-start = ((s8[4841472]{0:T(1024)(128)(4,1)}), s8[647168]{0:T(1024)(128)(4,1)S(1)}, s32[]{:S(2)}) async-start(s8[4841472]{0:T(1024)(128)(4,1)} %bitcast.71), calls=%async_computation.3 | async-start | bytes 1294336
  369.7 22.4 %slice-start.1 = ((s8[4841472]{0:T(1024)(128)(4,1)}), s8[4194304]{0:T(1024)(128)(4,1)S(1)}, s32[]{:S(2)}) async-start(s8[4841472]{0:T(1024)(128)(4,1)} %bitcast.71), calls=%async_computation.4 | async-start | bytes 8388608
  369.7 22.4 %copy-start.21 = (bf16[384,1536]{1,0:T(8,128)(2,1)S(1)}, bf16[384,1536]{1,0:T(8,128)(2,1)}, u32[]{:S(2)}) copy-start(bf16[384,1536]{1,0:T(8,128)(2,1)} %reshape.206) | copy-start | bytes 3538948
  392.1 11.6 %copy-start.9 = (f32[3152,384]{1,0:T(8,128)S(1)}, f32[3152,384]{1,0:T(8,128)}, u32[]{:S(2)}) copy-start(f32[3152,384]{1,0:T(8,128)} %reshape.209) | copy-start | bytes 14524420
  392.1 11.6 %copy-start.28 = (f32[3152]{0:T(1024)S(1)}, f32[3152]{0:T(1024)}, u32[]{:S(2)}) copy-start(f32[3152]{0:T(1024)} %mul.192) | copy-start | bytes 37828
  416.6 8.2 %copy-start.14 = (bf16[16,197,1,6,64]{1,4,3,0,2:T(8,128)(2,1)S(1)}, bf16[16,197,1,6,64]{1,4,3,0,2:T(8,128)(2,1)}, u32[]{:S(2)}) copy-start(bf16[16,197,1,6,64]{1,4,3,0,2:T(8,128)(2,1)} %copy-done.13) | copy-start | bytes 7262212
  416.6 8.2 %copy-start.25 = (f32[16,6,197]{2,1,0:T(8,128)S(1)}, f32[16,6,197]{2,1,0:T(8,128)}, u32[]{:S(2)}) copy-start(f32[16,6,197]{2,1,0:T(8,128)} %copy-done.24) | copy-start | bytes 226948
  439.0 18.0 %copy-start.4 = (bf16[16,197,1,6,64]{1,4,3,0,2:T(8,128)(2,1)S(1)}, bf16[16,197,1,6,64]{1,4,3,0,2:T(8,128)(2,1)}, u32[]{:S(2)}) copy-start(bf16[16,197,1,6,64]{1,4,3,0,2:T(8,128)(2,1)} %copy-done.3) | copy-start | bytes 7262212
  480.1 11.2 %copy-start.7 = (bf16[3152,384]{0,1:T(8,128)(2,1)S(1)}, bf16[3152,384]{0,1:T(8,128)(2,1)}, u32[]{:S(2)}) copy-start(bf16[3152,384]{0,1:T(8,128)(2,1)} %copy-done.6) | copy-start | bytes 7262212
  548.5 11.5 %copy-start.23 = (bf16[384,1152]{1,0:T(8,128)(2,1)S(1)}, bf16[384,1152]{1,0:T(8,128)(2,1)}, u32[]{:S(2)}) copy-start(bf16[384,1152]{1,0:T(8,128)(2,1)} %copy-done.22) | copy-start | bytes 2654212
  548.5 11.5 %copy-start.26 = (f32[3152]{0:T(1024)S(1)}, f32[3152]{0:T(1024)}, u32[]{:S(2)}) copy-start(f32[3152]{0:T(1024)} %rsqrt.22) | copy-start | bytes 37828
  548.5 11.5 %copy-start.27 = (f32[3152]{0:T(1024)S(1)}, f32[3152]{0:T(1024)}, u32[]{:S(2)}) copy-start(f32[3152]{0:T(1024)} %div.43) | copy-start | bytes 37828
  548.5 11.5 %copy-start.32 = (f32[384]{0:T(512)S(1)}, f32[384]{0:T(512)}, u32[]{:S(2)}) copy-start(f32[384]{0:T(512)} %copy-done.31) | copy-start | bytes 4612
  580.7 10.1 %slice-start.2 = ((s8[4841472]{0:T(1024)(128)(4,1)}), s8[647168]{0:T(1024)(128)(4,1)S(1)}, s32[]{:S(2)}) async-start(s8[4841472]{0:T(1024)(128)(4,1)} %bitcast.73), calls=%async_computation.5 | async-start | bytes 1294336
  (24 other events, 107.2 us)
Sparse Core Ops, SparseCore 0:
  11.0 56.9 all-gather.4
  71.0 53.8 all-gather.6
  572.2 162.9 all-reduce.8
where the time goes:
time: 755 us; the launch traced here: 748 us
  matrix products  215 us (28%)
  local copies, waits for them, and re-layouts  183 us (24%)
  blocking collectives  173 us (23%)
  waiting for transfers between devices  91.5 us (12%)
  other arithmetic  68.9 us (9%)
  between operations  16.8 us (2%)
    dot_general x12, matrix products, matmul(): return jnp.dot(left, right, preferred_element_type=jnp.float32)  155 us
    unnamed x4, waiting for transfers between devices  91.5 us
    unnamed x2, blocking collectives  82.4 us
    all_gather x1, blocking collectives, body(): lax.all_gather(qkv_flat, ('dp', 'fsdp'), axis=0, tiled=True)  51.2 us
    unnamed x112, local copies, waits for them, and re-layouts  42.2 us
    all_gather x1, blocking collectives, body(): lax.all_gather(out_flat, ('dp', 'fsdp'), axis=0, tiled=True)  39.1 us
    sub x1, other arithmetic, body(): weights_exp = jnp.exp(scores - row_max)  22.3 us
    reshape x1, local copies, waits for them, and re-layouts, body(): projected = projected.reshape(slot_count, length, 3, HEADS, HD)  22.3 us
  transfers between devices with their start and end apart: 3, of which 1 were waited for; matrix products, arithmetic and copies ran while one was open for 34% of the time, Pallas kernels for 0%

commit v1 on v0

v1 whole, which is shorter than its diff:
```python
import functools

import jax
import jax.numpy as jnp
from jax import lax
from jax.experimental import pallas as pl
from jax.experimental.pallas import tpu as pltpu
from jax.sharding import PartitionSpec as P

D = 384
HEADS = 6
HD = 64
FF = 1536
EPS = 1e-06
AXES = ("dp", "fsdp")
GROUP = 2
CHUNK = 384
PAIR = 2 * HD
F32 = jnp.float32
BF16 = jnp.bfloat16


def dot(a, b, contract=((1,), (0,))):
    return lax.dot_general(a, b, (contract, ((), ())), preferred_element_type=F32)


def dot_t(a, b):
    return dot(a, b, ((1,), (1,)))


def normalize(rows):
    center = rows - jnp.mean(rows, axis=-1, keepdims=True)
    inverse = lax.rsqrt(jnp.mean(center * center, axis=-1, keepdims=True) + EPS)
    return center * inverse, inverse


def norm_back(upstream, normed, inverse, gain):
    scaled = upstream * gain
    first = jnp.mean(scaled, axis=-1, keepdims=True)
    second = jnp.mean(scaled * normed, axis=-1, keepdims=True)
    return inverse * (scaled - first - normed * second)


def column_sum(rows):
    return jnp.sum(rows, axis=0, keepdims=True)


def kernel(
    length, padded, counts, x_ref, ct_ref, wqkv, wout, wup, wdown, vec,
    block_out, input_grad, gqkv, gout, gup, gdown, gvec,
    aqkv, aout, aup, adown, avec, xs, es, qkv_s, mix_s, dmix_s, dqkv_s, p_s,
):
    step = pl.program_id(0)

    @pl.when(step == 0)
    def _():
        for ref in (aqkv, aout, aup, adown, avec, xs, es):
            ref[...] = jnp.zeros_like(ref)

    count = counts[0]
    for i in range(GROUP):
        valid = (step * GROUP + i < count).astype(F32)
        xs[i * padded : i * padded + length, :] = x_ref[i].astype(F32)
        es[i * padded : i * padded + length, :] = ct_ref[i].astype(F32) * valid

    def piece(k):
        return vec[:, k * D : (k + 1) * D]

    g1, c1, g2, c2, bq, bv, bo, bd = [piece(k) for k in range(8)]
    bias = jnp.concatenate([bq, jnp.zeros_like(bq), bv], axis=1)

    def add_vec(k, rows):
        avec[:, k * D : (k + 1) * D] += rows

    n1, inv1 = normalize(xs[...])
    a1 = (n1 * g1 + c1).astype(BF16)
    qkv_s[...] = (dot(a1, wqkv[...]) + bias).astype(BF16)

    first_half = lax.broadcasted_iota(jnp.int32, (padded, PAIR), 1) < HD
    key_ok = lax.broadcasted_iota(jnp.int32, (2 * padded, padded), 1) < length

    def stack(rows):
        zero = jnp.zeros_like(rows)
        return jnp.concatenate(
            [jnp.where(first_half, rows, zero), jnp.where(first_half, zero, rows)], axis=0
        )

    def unstack(rows):
        return jnp.where(first_half, rows[:padded], rows[padded:])

    def part(ref, i, which, pair):
        start = which * D + pair * PAIR
        return ref[i * padded : (i + 1) * padded, start : start + PAIR]

    scale = HD ** (-0.5)
    for i in range(GROUP):
        for pair in range(HEADS // 2):
            q = stack(part(qkv_s, i, 0, pair) * scale)
            scores = dot_t(q, part(qkv_s, i, 1, pair))
            scores = jnp.where(key_ok, scores, -1e30)
            e = jnp.exp(scores - jnp.max(scores, axis=-1, keepdims=True))
            p = e * (1.0 / jnp.sum(e, axis=-1, keepdims=True))
            p_s[i * (HEADS // 2) + pair] = p
            mixed = dot(p.astype(BF16), part(qkv_s, i, 2, pair))
            mix_s[i * padded : (i + 1) * padded, pair * PAIR : (pair + 1) * PAIR] = unstack(
                mixed
            ).astype(BF16)

    mix = mix_s[...]
    residual = xs[...] + dot(mix, wout[...]) + bo
    n2, inv2 = normalize(residual)
    a2 = (n2 * g2 + c2).astype(BF16)
    a2_t = a2.T
    e_low = es[...].astype(BF16)
    e_low_t = e_low.T
    total = residual + bd
    back = jnp.zeros_like(total)
    for c in range(FF // CHUNK):
        cols = slice(c * CHUNK, (c + 1) * CHUNK)
        vcols = slice(8 * D + c * CHUNK, 8 * D + (c + 1) * CHUNK)
        u = dot(a2, wup[:, cols]) + vec[:, vcols]
        cdf = 0.5 + 0.5 * lax.erf(u * (0.5**0.5))
        act = (u * cdf).astype(BF16)
        pdf = jnp.exp(-0.5 * u * u) * 0.3989422804014327
        du = dot_t(e_low, wdown[cols, :]) * (cdf + u * pdf)
        du_low = du.astype(BF16)
        total = total + dot(act, wdown[cols, :])
        back = back + dot_t(du_low, wup[:, cols])
        aup[:, cols] += dot(a2_t, du_low)
        adown[:, cols] += dot(e_low_t, act)
        avec[:, vcols] += column_sum(du_low.astype(F32))
    for i in range(GROUP):
        keep = step * GROUP + i < count
        rows = total[i * padded : i * padded + length]
        block_out[i] = jnp.where(keep, rows, 0.0).astype(BF16)
    add_vec(7, column_sum(e_low.astype(F32)))
    add_vec(2, column_sum(back * n2))
    add_vec(3, column_sum(back))
    dr = es[...] + norm_back(back, n2, inv2, g2)
    dr_low = dr.astype(BF16)
    es[...] = dr
    aout[...] += dot(mix.T, dr_low)
    add_vec(6, column_sum(dr_low.astype(F32)))
    dmix_s[...] = dot_t(dr_low, wout[...]).astype(BF16)

    for i in range(GROUP):
        rows = slice(i * padded, (i + 1) * padded)
        for pair in range(HEADS // 2):
            q = stack(part(qkv_s, i, 0, pair) * scale)
            k = part(qkv_s, i, 1, pair)
            do = stack(part(dmix_s, i, 0, pair))
            p = p_s[i * (HEADS // 2) + pair]
            dp = dot_t(do, part(qkv_s, i, 2, pair))
            ds = (p * (dp - jnp.sum(dp * p, axis=-1, keepdims=True))).astype(BF16)
            dv = dot(p.astype(BF16).T, do)
            dk = dot(ds.T, q)
            dq = unstack(dot(ds, k)) * scale
            for which, value in enumerate((dq, dk, dv)):
                start = which * D + pair * PAIR
                dqkv_s[rows, start : start + PAIR] = value.astype(BF16)

    dqkv = dqkv_s[...]
    aqkv[...] += dot(a1.T, dqkv)
    add_vec(4, column_sum(dqkv[:, :D].astype(F32)))
    add_vec(5, column_sum(dqkv[:, 2 * D :].astype(F32)))
    back1 = dot_t(dqkv, wqkv[...])
    add_vec(0, column_sum(back1 * n1))
    add_vec(1, column_sum(back1))
    dx = es[...] + norm_back(back1, n1, inv1, g1)
    for i in range(GROUP):
        input_grad[i] = dx[i * padded : i * padded + length]
    for i in range(GROUP):
        es[i * padded + length : (i + 1) * padded, :] = jnp.zeros((padded - length, D), F32)

    @pl.when(step == pl.num_programs(0) - 1)
    def _():
        gqkv[...] = aqkv[...].astype(BF16)
        gout[...] = aout[...].astype(BF16)
        gup[...] = aup[...].astype(BF16)
        gdown[...] = adown[...].T.astype(BF16)
        gvec[...] = avec[...]


def block(images, counts, weights, vec, cotangent):
    slots, length, _ = images.shape
    padded = -(-length // 16) * 16
    rows = GROUP * padded
    image_spec = pl.BlockSpec((GROUP, length, D), lambda s: (s, 0, 0))

    def whole(shape):
        return pl.BlockSpec(shape, lambda s: (0, 0))

    shapes = [(D, 3 * D), (D, D), (D, FF), (FF, D)]
    vec_shape = (1, 8 * D + FF)
    flops = 3 * 2 * slots * length * (3 * D * D + D * D + 2 * D * FF)
    return pl.pallas_call(
        functools.partial(kernel, length, padded),
        grid=(slots // GROUP,),
        in_specs=[pl.BlockSpec(memory_space=pltpu.SMEM), image_spec, image_spec]
        + [whole(s) for s in shapes]
        + [whole(vec_shape)],
        out_specs=[image_spec, image_spec] + [whole(s) for s in shapes] + [whole(vec_shape)],
        out_shape=[
            jax.ShapeDtypeStruct(images.shape, BF16),
            jax.ShapeDtypeStruct(images.shape, F32),
        ]
        + [jax.ShapeDtypeStruct(s, BF16) for s in shapes]
        + [jax.ShapeDtypeStruct(vec_shape, F32)],
        scratch_shapes=[
            pltpu.VMEM((D, 3 * D), F32),
            pltpu.VMEM((D, D), F32),
            pltpu.VMEM((D, FF), F32),
            pltpu.VMEM((D, FF), F32),
            pltpu.VMEM(vec_shape, F32),
            pltpu.VMEM((rows, D), F32),
            pltpu.VMEM((rows, D), F32),
            pltpu.VMEM((rows, 3 * D), BF16),
            pltpu.VMEM((rows, D), BF16),
            pltpu.VMEM((rows, D), BF16),
            pltpu.VMEM((rows, 3 * D), BF16),
            pltpu.VMEM((GROUP * HEADS // 2, 2 * padded, padded), F32),
        ],
        compiler_params=pltpu.CompilerParams(vmem_limit_bytes=56 * 2**20),
        cost_estimate=pl.CostEstimate(flops=flops, bytes_accessed=20 * 2**20, transcendentals=0),
    )(counts, images, cotangent, *weights, vec)


def stage_orders(dp, fsdp):
    inner = fsdp.bit_length() - 1
    outer = dp.bit_length() - 1
    z = list(range(1, inner))
    near = list(range(inner, inner + outer // 2))
    far = list(range(inner + outer // 2, inner + outer))
    return ([0] + near + far + z, [0] + far + z + near, [0] + z + near + far), inner + outer


def swap(value, bit, devices):
    return lax.ppermute(value, AXES, [(d, d ^ (1 << bit)) for d in range(devices)])


def gather(value, order, bits, me):
    held = value.reshape((1,) * bits + value.shape)
    for bit in reversed(order):
        other = swap(held, bit, 1 << bits)
        axis = bits - 1 - bit
        upper = (me >> bit) & 1
        held = jnp.where(
            upper == 1,
            jnp.concatenate([other, held], axis=axis),
            jnp.concatenate([held, other], axis=axis),
        )
    return held.reshape((1 << bits,) + value.shape)


def reduce_scatter(value, order, bits, me):
    held = value.reshape((2,) * bits + value.shape[1:])
    for bit in order:
        axis = bits - 1 - bit
        upper = (me >> bit) & 1
        sent = lax.dynamic_index_in_dim(held, 1 - upper, axis, keepdims=True)
        kept = lax.dynamic_index_in_dim(held, upper, axis, keepdims=True)
        got = swap(sent.astype(BF16), bit, 1 << bits)
        total = kept.astype(F32) + got.astype(F32)
        held = total if bit == order[-1] else total.astype(BF16)
    return held.reshape(value.shape[1:])


def make_body(dp, fsdp):
    devices = dp * fsdp
    orders, bits = stage_orders(dp, fsdp)
    rows_each = D // devices if D % devices == 0 else None

    def body(images, counts, qkv_flat, out_flat, up_flat, down_flat, vectors, cotangent):
        me = lax.axis_index(AXES)

        def shard(flat, width):
            return flat if rows_each is None else flat.reshape(rows_each, width)

        first = jnp.concatenate([shard(qkv_flat, 3 * D), shard(out_flat, D)], axis=-1)
        parts = [first, shard(up_flat, FF), shard(down_flat, FF)]
        first, up, down = [gather(v, o, bits, me) for v, o in zip(parts, orders)]
        vec = gather(vectors, orders[0], bits, me)
        cut = qkv_flat.shape[0] if rows_each is None else 3 * D
        weights = [
            first[..., :cut].reshape(D, 3 * D),
            first[..., cut:].reshape(D, D),
            up.reshape(D, FF),
            down.reshape(FF, D),
        ]
        vec = vec.astype(F32).reshape(1, -1)
        block_out, input_grad, gqkv, gout, gup, gdown, gvec = block(
            images, counts, weights, vec, cotangent
        )

        def blocks(grad, width):
            if rows_each is None:
                return grad.reshape(devices, -1)
            return grad.reshape(devices, rows_each, width)

        gfirst = jnp.concatenate([blocks(gqkv, 3 * D), blocks(gout, D)], axis=-1)
        grads = [gfirst, blocks(gup, FF), blocks(gdown, FF)]
        gfirst, gup, gdown = [reduce_scatter(g, o, bits, me) for g, o in zip(grads, orders)]
        gvec = reduce_scatter(gvec.reshape(devices, -1), orders[0], bits, me)
        return (
            block_out,
            input_grad,
            gfirst[..., :cut].reshape(-1),
            gfirst[..., cut:].reshape(-1),
            gup.reshape(-1),
            gdown.reshape(-1),
            gvec,
        )

    return body


def solution(mesh):
    split = P(AXES)
    image = P(AXES, None, None)
    return jax.shard_map(
        make_body(mesh.shape["dp"], mesh.shape["fsdp"]),
        mesh=mesh,
        in_specs=(image, split, split, split, split, split, split, image),
        out_specs=(image, image, split, split, split, split, split),
        check_vma=False,
    )
```

time: 755 us -> 271 us (0.36)
  matrix products: 215 us -> 0 us
  blocking collectives: 173 us -> 0 us
  local copies, waits for them, and re-layouts: 183 us -> 57.7 us
  Pallas kernels: 0 us -> 108 us
  other arithmetic: 68.9 us -> 8.28 us
  starting transfers between devices: 0.11 us -> 37.8 us
  waiting for transfers between devices: 91.5 us -> 56.4 us
  between operations: 16.8 us -> 1.97 us
    dot_general x18 -> x0, matrix products: 215 us -> none  [the longest x12 155 us: matmul(): return jnp.dot(left, right, preferred_element_type=jnp.float32)]
    pallas_call x0 -> x1, Pallas kernels: none -> 108 us  [block(): pl.pallas_call(functools.partial(kernel, length, padded), grid=(slots //...]
    unnamed x4 -> x0, waiting for transfers between devices: 91.5 us -> none
    all_gather x2 -> x0, blocking collectives: 90.2 us -> none  [the longest x1 51.2 us: body(): lax.all_gather(qkv_flat, ('dp', 'fsdp'), axis=0, tiled=True)]
    unnamed x2 -> x0, blocking collectives: 82.4 us -> none
    reshape x16 -> x7, local copies, waits for them, and re-layouts: 74.3 us -> 5.32 us  [the longest x2 1.53 us: shard(): return flat if rows_each is None else flat.reshape(rows_each, width)]
    ppermute x0 -> x40, waiting for transfers between devices: none -> 56.4 us  [swap(): lax.ppermute(value, AXES, [(d, d ^ 1 << bit) for d in range(devices)])]
    ppermute x0 -> x40, starting transfers between devices: none -> 37.8 us  [swap(): lax.ppermute(value, AXES, [(d, d ^ 1 << bit) for d in range(devices)])]
  transfers between devices with their start and end apart: 3 -> 40, of which waited for: 1 -> 15; matrix products, arithmetic and copies ran while one was open for 34% -> 21% of each run, Pallas kernels for 0% -> 0%
where the time goes in v1:
time: 271 us; the launch traced here: 270 us
  Pallas kernels  108 us (40%)
  local copies, waits for them, and re-layouts  57.7 us (21%)
  waiting for transfers between devices  56.4 us (21%)
  starting transfers between devices  37.8 us (14%)
  other arithmetic  8.28 us (3%)
    pallas_call x1, Pallas kernels, block(): pl.pallas_call(functools.partial(kernel, length, padded), grid=(slots //...  108 us
    ppermute x40, waiting for transfers between devices, swap(): lax.ppermute(value, AXES, [(d, d ^ 1 << bit) for d in range(devices)])  56.4 us
    ppermute x40, starting transfers between devices, swap(): lax.ppermute(value, AXES, [(d, d ^ 1 << bit) for d in range(devices)])  37.8 us
    unnamed x14, local copies, waits for them, and re-layouts  16.6 us
    select_n x9, local copies, waits for them, and re-layouts, gather(): jnp.where(upper == 1, jnp.concatenate([other, held], axis=axis), jnp.conc...  12.5 us
    dynamic_slice x22, local copies, waits for them, and re-layouts, reduce_scatter(): sent = lax.dynamic_index_in_dim(held, 1 - upper, axis, keepdims=True)  5.68 us
  transfers between devices with their start and end apart: 40, of which 15 were waited for; matrix products, arithmetic and copies ran while one was open for 21% of the time, Pallas kernels for 0%

profile of v1, /device:TPU:0, one launch (start us, length us, event | category | flops | bytes accessed | tf_op | source)
XLA Modules:
  0.0 269.8 jit_solution(12566835514223019944)
XLA Ops:
  1.5 3.0 %collective-permute-start.5 = (bf16[1,1,1,1,1,12,1536]{6,5,4,3,2,1,0:T(8,128)(2,1)S(1)}, bf16[1,1,1,1,1,12,1536]{6,5,4,3,2,1,0:T(8,128)(2,1)S(1)}, u32[]{:S(2)}, u32[]{:S(2)}) collective-permute-start(bf16[1,1,1,1,1,12,1536]{6,5,4,3,2,1,0:T(8,128)(2,1)S(1)} %reshape_reshape.23), channel_id=1, source_target_pairs={{0,8},{1,9},{2,10},{3,11},{4,12},{5,13},{6,14},{7,15},{8,0},{9,1},... | collective-permute-start | bytes 110600 | tf_op jit(solution)/shard_map/ppermute | solution.py:238
  8.5 2.7 collective-permute-start
  14.5 3.8 %copy.200.x_ref = bf16[16,197,384]{2,1,0:T(8,128)(2,1)} copy(bf16[16,197,384]{2,0,1:T(8,128)(2,1)} %param.8) | data formatting | bytes 4841472 | tf_op args[0]
  25.2 3.0 %collective-permute-done.17 = bf16[1,1,2,2,1,144]{5,2,3,4,1,0:T(2,128)(2,1)S(1)} collective-permute-done((bf16[1,1,2,2,1,144]{5,2,3,4,1,0:T(2,128)(2,1)S(1)}, bf16[1,1,2,2,1,144]{5,2,3,4,1,0:T(2,128)(2,1)S(1)}, u32[]{:S(2)}, u32[]{:S(2)}) %collective-permute-start.17) | collective-permute-done | bytes 1184 | tf_op jit(solution)/shard_map/ppermute | solution.py:238
  28.9 3.1 %collective-permute-done.18 = bf16[2,1,2,2,1,144]{5,2,3,4,1,0:T(2,128)(2,1)S(1)} collective-permute-done((bf16[2,1,2,2,1,144]{5,2,3,4,1,0:T(2,128)(2,1)S(1)}, bf16[2,1,2,2,1,144]{5,2,3,4,1,0:T(2,128)(2,1)S(1)}, u32[]{:S(2)}, u32[]{:S(2)}) %collective-permute-start.18) | collective-permute-done | bytes 2336 | tf_op jit(solution)/shard_map/ppermute | solution.py:238
  32.1 2.7 collective-permute-start.6
  37.2 3.3 %collective-permute-done.6 = bf16[1,2,1,1,1,12,1536]{6,5,2,3,0,4,1:T(8,128)(2,1)S(1)} collective-permute-done((bf16[1,2,1,1,1,12,1536]{6,5,2,3,0,4,1:T(8,128)(2,1)S(1)}, bf16[1,2,1,1,1,12,1536]{6,5,2,3,0,4,1:T(8,128)(2,1)S(1)}, u32[]{:S(2)}, u32[]{:S(2)}) %collective-permute-start.6) | collective-permute-done | bytes 73760 | tf_op jit(solution)/shard_map/ppermute | solution.py:238
  41.4 3.4 %collective-permute-start.12 = (bf16[2,2,1,1,1,12,1536]{6,5,2,3,0,4,1:T(8,128)(2,1)S(1)}, bf16[2,2,1,1,1,12,1536]{6,5,2,3,0,4,1:T(8,128)(2,1)S(1)}, u32[]{:S(2)}, u32[]{:S(2)}) collective-permute-start(bf16[2,2,1,1,1,12,1536]{6,5,2,3,0,4,1:T(8,128)(2,1)S(1)} %fusion.3), channel_id=1, source_target_pairs={{0,4},{1,5},{2,6},{3,7},{4,0},{5,1},{6,2},{7,3},{8,12},{9,13},{10,... | collective-permute-start | bytes 442376 | tf_op jit(solution)/shard_map/ppermute | solution.py:238
  45.6 5.5 %collective-permute-done.7 = bf16[1,2,2,1,1,12,1536]{6,5,2,3,0,4,1:T(8,128)(2,1)S(1)} collective-permute-done((bf16[1,2,2,1,1,12,1536]{6,5,2,3,0,4,1:T(8,128)(2,1)S(1)}, bf16[1,2,2,1,1,12,1536]{6,5,2,3,0,4,1:T(8,128)(2,1)S(1)}, u32[]{:S(2)}, u32[]{:S(2)}) %collective-permute-start.7) | collective-permute-done | bytes 147488 | tf_op jit(solution)/shard_map/ppermute | solution.py:238
  51.7 2.2 collective-permute-done.12
  55.3 9.4 %collective-permute-done.3 = bf16[2,1,2,2,1,12,1536]{6,5,2,3,0,4,1:T(8,128)(2,1)S(1)} collective-permute-done((bf16[2,1,2,2,1,12,1536]{6,5,2,3,0,4,1:T(8,128)(2,1)S(1)}, bf16[2,1,2,2,1,12,1536]{6,5,2,3,0,4,1:T(8,128)(2,1)S(1)}, u32[]{:S(2)}, u32[]{:S(2)}) %collective-permute-start.3) | collective-permute-done | bytes 294944 | tf_op jit(solution)/shard_map/ppermute | solution.py:238
  72.5 2.2 copy.163
  74.7 2.9 %select_n.715 = bf16[32,12,1536]{2,0,1:T(8,128)(2,1)S(1)} reshape(bf16[2,2,2,2,2,12,1536]{6,4,3,2,1,0,5:T(2,128)(2,1)} %copy.163) | data formatting | bytes 2359296 | tf_op jit(solution)/shard_map/jit(_where)/select_n | solution.py:247
  86.0 107.7 %shard_map.135 = (bf16[16,197,384]{2,1,0:T(8,128)(2,1)}, f32[16,197,384]{2,1,0:T(8,128)}, bf16[384,1152]{1,0:T(8,128)(2,1)}, bf16[384,384]{1,0:T(8,128)(2,1)}, b...) custom-call(s32[1]{0:T(128)S(6)} %copy.241.counts, bf16[16,197,384]{2,1,0:T(8,128)(2,1)} %copy.200.x_ref, ...), custom_call_target="tpu_custom_call" | custom-call | flops 33464254464 | bytes 20971520 | tf_op jit(solution)/shard_map/pallas_call | solution.py:196
  195.2 2.4 reshape_reshape.27
  199.1 2.1 reshape_reshape.25
  203.2 2.2 concatenate.1160
  206.5 2.4 constant_dynamic-update-slice_fusion.3
  212.2 2.3 collective-permute-done.37
  218.1 2.5 collective-permute-start.39
  220.6 5.7 %copy.209 = f32[16,197,384]{2,0,1:T(8,128)} copy(f32[16,197,384]{2,1,0:T(8,128)} %get-tuple-element.50) | data formatting | bytes 9682944
  234.1 7.4 %collective-permute-done.31 = bf16[2,2,2,1,1,12,1536]{6,5,4,3,2,1,0:T(8,128)(2,1)S(1)} collective-permute-done((bf16[2,2,2,1,1,12,1536]{6,5,4,3,2,1,0:T(8,128)(2,1)S(1)}, bf16[2,2,2,1,1,12,1536]{6,5,4,3,2,1,0:T(8,128)(2,1)S(1)}, u32[]{:S(2)}, u32[]{:S(2)}) %collective-permute-start.31) | collective-permute-done | bytes 294944 | tf_op jit(solution)/shard_map/ppermute | solution.py:238
  245.6 7.7 %collective-permute-done.32 = bf16[2,2,1,1,1,12,1536]{6,5,4,3,2,1,0:T(8,128)(2,1)S(1)} collective-permute-done((bf16[2,2,1,1,1,12,1536]{6,5,4,3,2,1,0:T(8,128)(2,1)S(1)}, bf16[2,2,1,1,1,12,1536]{6,5,4,3,2,1,0:T(8,128)(2,1)S(1)}, u32[]{:S(2)}, u32[]{:S(2)}) %collective-permute-start.32) | collective-permute-done | bytes 147488 | tf_op jit(solution)/shard_map/ppermute | solution.py:238
  262.9 4.4 %collective-permute-done.24 = bf16[1,1,1,1,1,12,1536]{6,5,4,3,2,1,0:T(8,128)(2,1)S(1)} collective-permute-done((bf16[1,1,1,1,1,12,1536]{6,5,4,3,2,1,0:T(8,128)(2,1)S(1)}, bf16[1,1,1,1,1,12,1536]{6,5,4,3,2,1,0:T(8,128)(2,1)S(1)}, u32[]{:S(2)}, u32[]{:S(2)}) %collective-permute-start.24) | collective-permute-done | bytes 36896 | tf_op jit(solution)/shard_map/ppermute | solution.py:238
  (193 shorter events, 73.9 us)
Async XLA Ops:
  1.5 30.6 %collective-permute-start.5 = (bf16[1,1,1,1,1,12,1536]{6,5,4,3,2,1,0:T(8,128)(2,1)S(1)}, bf16[1,1,1,1,1,12,1536]{6,5,4,3,2,1,0:T(8,128)(2,1)S(1)}, u32[]{:S(2)}, u32[]{:S(2)}) collective-permute-start(bf16[1,1,1,1,1,12,1536]{6,5,4,3,2,1,0:T(8,128)(2,1)S(1)} %reshape_reshape.23), channel_id=1, source_target_pairs={{0,8},{1,9},{2,10},{3,11},{4,12},{5,13},{6,14},{7,15},{8,0},{9,1},... | collective-permute-start | bytes 110600 | tf_op jit(solution)/shard_map/ppermute | solution.py:238
  5.3 29.5 %collective-permute-start.10 = (bf16[1,1,1,1,1,12,1536]{6,5,0,4,3,2,1:T(8,128)(2,1)S(1)}, bf16[1,1,1,1,1,12,1536]{6,5,0,4,3,2,1:T(8,128)(2,1)S(1)}, u32[]{:S(2)}, u32[]{:S(2)}) collective-permute-start(bf16[1,1,1,1,1,12,1536]{6,5,0,4,3,2,1:T(8,128)(2,1)S(1)} %reshape_reshape.24), channel_id=1, source_target_pairs={{0,16},{1,17},{2,18},{3,19},{4,20},{5,21},{6,22},{7,23},{8,24},{9,... | collective-permute-start | bytes 110600 | tf_op jit(solution)/shard_map/ppermute | solution.py:238
  8.5 27.0 %collective-permute-start = (bf16[1,1,1,1,1,12,1536]{6,5,2,3,0,4,1:T(8,128)(2,1)S(1)}, bf16[1,1,1,1,1,12,1536]{6,5,2,3,0,4,1:T(8,128)(2,1)S(1)}, u32[]{:S(2)}, u32[]{:S(2)}) collective-permute-start(bf16[1,1,1,1,1,12,1536]{6,5,2,3,0,4,1:T(8,128)(2,1)S(1)} %bitcast.105), channel_id=1, source_target_pairs={{0,4},{1,5},{2,6},{3,7},{4,0},{5,1},{6,2},{7,3},{8,12},{9,13},{10,... | collective-permute-start | bytes 110600 | tf_op jit(solution)/shard_map/ppermute | solution.py:238
  32.0 38.1 %collective-permute-start.19 = (bf16[2,2,2,2,1,144]{5,2,3,4,1,0:T(2,128)(2,1)S(1)}, bf16[2,2,2,2,1,144]{5,2,3,4,1,0:T(2,128)(2,1)S(1)}, u32[]{:S(2)}, u32[]{:S(2)}) collective-permute-start(bf16[2,2,2,2,1,144]{5,2,3,4,1,0:T(2,128)(2,1)S(1)} %broadcast_select_fusion.1), channel_id=1, source_target_pairs={{0,1},{1,0},{2,3},{3,2},{4,5},{5,4},{6,7},{7,6},{8,9},{9,8},{10,11... | collective-permute-start | bytes 13832 | tf_op jit(solution)/shard_map/ppermute | solution.py:238
  35.4 9.4 %collective-permute-start.1 = (bf16[1,1,2,1,1,12,1536]{6,5,2,3,0,4,1:T(8,128)(2,1)S(1)}, bf16[1,1,2,1,1,12,1536]{6,5,2,3,0,4,1:T(8,128)(2,1)S(1)}, u32[]{:S(2)}, u32[]{:S(2)}) collective-permute-start(bf16[1,1,2,1,1,12,1536]{6,5,2,3,0,4,1:T(8,128)(2,1)S(1)} %maximum_select_fusion.18), channel_id=1, source_target_pairs={{0,2},{1,3},{2,0},{3,1},{4,6},{5,7},{6,4},{7,5},{8,10},{9,11},{10,... | collective-permute-start | bytes 221192 | tf_op jit(solution)/shard_map/ppermute | solution.py:238
  40.7 10.3 %collective-permute-start.7 = (bf16[1,2,2,1,1,12,1536]{6,5,2,3,0,4,1:T(8,128)(2,1)S(1)}, bf16[1,2,2,1,1,12,1536]{6,5,2,3,0,4,1:T(8,128)(2,1)S(1)}, u32[]{:S(2)}, u32[]{:S(2)}) collective-permute-start(bf16[1,2,2,1,1,12,1536]{6,5,2,3,0,4,1:T(8,128)(2,1)S(1)} %maximum_select_fusion.14), channel_id=1, source_target_pairs={{0,2},{1,3},{2,0},{3,1},{4,6},{5,7},{6,4},{7,5},{8,10},{9,11},{10,... | collective-permute-start | bytes 442376 | tf_op jit(solution)/shard_map/ppermute | solution.py:238
  41.4 12.5 %collective-permute-start.12 = (bf16[2,2,1,1,1,12,1536]{6,5,2,3,0,4,1:T(8,128)(2,1)S(1)}, bf16[2,2,1,1,1,12,1536]{6,5,2,3,0,4,1:T(8,128)(2,1)S(1)}, u32[]{:S(2)}, u32[]{:S(2)}) collective-permute-start(bf16[2,2,1,1,1,12,1536]{6,5,2,3,0,4,1:T(8,128)(2,1)S(1)} %fusion.3), channel_id=1, source_target_pairs={{0,4},{1,5},{2,6},{3,7},{4,0},{5,1},{6,2},{7,3},{8,12},{9,13},{10,... | collective-permute-start | bytes 442376 | tf_op jit(solution)/shard_map/ppermute | solution.py:238
  44.9 9.4 %collective-permute-start.2 = (bf16[1,1,2,2,1,12,1536]{6,5,2,3,0,4,1:T(8,128)(2,1)S(1)}, bf16[1,1,2,2,1,12,1536]{6,5,2,3,0,4,1:T(8,128)(2,1)S(1)}, u32[]{:S(2)}, u32[]{:S(2)}) collective-permute-start(bf16[1,1,2,2,1,12,1536]{6,5,2,3,0,4,1:T(8,128)(2,1)S(1)} %maximum_select_fusion.12), channel_id=1, source_target_pairs={{0,16},{1,17},{2,18},{3,19},{4,20},{5,21},{6,22},{7,23},{8,24},{9,... | collective-permute-start | bytes 442376 | tf_op jit(solution)/shard_map/ppermute | solution.py:238
  51.2 15.2 %collective-permute-start.8 = (bf16[1,2,2,2,1,12,1536]{6,5,2,3,0,4,1:T(8,128)(2,1)S(1)}, bf16[1,2,2,2,1,12,1536]{6,5,2,3,0,4,1:T(8,128)(2,1)S(1)}, u32[]{:S(2)}, u32[]{:S(2)}) collective-permute-start(bf16[1,2,2,2,1,12,1536]{6,5,2,3,0,4,1:T(8,128)(2,1)S(1)} %maximum_select_fusion.8), channel_id=1, source_target_pairs={{0,16},{1,17},{2,18},{3,19},{4,20},{5,21},{6,22},{7,23},{8,24},{9,... | collective-permute-start | bytes 884744 | tf_op jit(solution)/shard_map/ppermute | solution.py:238
  54.1 14.4 %collective-permute-start.13 = (bf16[2,2,2,1,1,12,1536]{6,5,2,3,0,4,1:T(8,128)(2,1)S(1)}, bf16[2,2,2,1,1,12,1536]{6,5,2,3,0,4,1:T(8,128)(2,1)S(1)}, u32[]{:S(2)}, u32[]{:S(2)}) collective-permute-start(bf16[2,2,2,1,1,12,1536]{6,5,2,3,0,4,1:T(8,128)(2,1)S(1)} %maximum_select_fusion.10), channel_id=1, source_target_pairs={{0,2},{1,3},{2,0},{3,1},{4,6},{5,7},{6,4},{7,5},{8,10},{9,11},{10,... | collective-permute-start | bytes 884744 | tf_op jit(solution)/shard_map/ppermute | solution.py:238
  54.5 10.3 %collective-permute-start.3 = (bf16[2,1,2,2,1,12,1536]{6,5,2,3,0,4,1:T(8,128)(2,1)S(1)}, bf16[2,1,2,2,1,12,1536]{6,5,2,3,0,4,1:T(8,128)(2,1)S(1)}, u32[]{:S(2)}, u32[]{:S(2)}) collective-permute-start(bf16[2,1,2,2,1,12,1536]{6,5,2,3,0,4,1:T(8,128)(2,1)S(1)} %maximum_select_fusion.6), channel_id=1, source_target_pairs={{0,8},{1,9},{2,10},{3,11},{4,12},{5,13},{6,14},{7,15},{8,0},{9,1},... | collective-permute-start | bytes 884744 | tf_op jit(solution)/shard_map/ppermute | solution.py:238
  68.0 9.7 %collective-permute-start.9 = (bf16[2,2,2,2,1,12,1536]{6,3,5,4,2,1,0:T(2,128)(2,1)}, bf16[2,2,2,2,1,12,1536]{6,3,5,4,2,1,0:T(2,128)(2,1)S(1)}, u32[]{:S(2)}, u32[]{:S(2)}) collective-permute-start(bf16[2,2,2,2,1,12,1536]{6,3,5,4,2,1,0:T(2,128)(2,1)} %copy.179), channel_id=1, source_target_pairs={{0,1},{1,0},{2,3},{3,2},{4,5},{5,4},{6,7},{7,6},{8,9},{9,8},{10,11... | collective-permute-start | bytes 1769480 | tf_op jit(solution)/shard_map/ppermute | solution.py:238
  70.1 10.2 %collective-permute-start.14 = (bf16[2,2,2,2,1,12,1536]{6,3,5,4,2,1,0:T(2,128)(2,1)}, bf16[2,2,2,2,1,12,1536]{6,3,5,4,2,1,0:T(2,128)(2,1)}, u32[]{:S(2)}, u32[]{:S(2)}) collective-permute-start(bf16[2,2,2,2,1,12,1536]{6,3,5,4,2,1,0:T(2,128)(2,1)} %copy.192), channel_id=1, source_target_pairs={{0,1},{1,0},{2,3},{3,2},{4,5},{5,4},{6,7},{7,6},{8,9},{9,8},{10,11... | collective-permute-start | bytes 1769480 | tf_op jit(solution)/shard_map/ppermute | solution.py:238
  194.6 10.8 %collective-permute-start.35 = (bf16[2,2,2,2,1,144]{5,4,3,2,1,0:T(2,128)(2,1)S(1)}, bf16[2,2,2,2,1,144]{5,4,3,2,1,0:T(2,128)(2,1)S(1)}, u32[]{:S(2)}, u32[]{:S(2)}) collective-permute-start(bf16[2,2,2,2,1,144]{5,4,3,2,1,0:T(2,128)(2,1)S(1)} %dynamic-slice_convert_fusion), channel_id=1, source_target_pairs={{0,1},{1,0},{2,3},{3,2},{4,5},{5,4},{6,7},{7,6},{8,9},{9,8},{10,11... | collective-permute-start | bytes 13832 | tf_op jit(solution)/shard_map/ppermute | solution.py:238
  199.1 29.6 %collective-permute-start.30 = (bf16[2,2,2,2,1,12,1536]{6,3,5,4,2,1,0:T(2,128)(2,1)}, bf16[2,2,2,2,1,12,1536]{6,3,5,4,2,1,0:T(2,128)(2,1)}, u32[]{:S(2)}, u32[]{:S(2)}) collective-permute-start(bf16[2,2,2,2,1,12,1536]{6,3,5,4,2,1,0:T(2,128)(2,1)} %copy.206), channel_id=1, source_target_pairs={{0,1},{1,0},{2,3},{3,2},{4,5},{5,4},{6,7},{7,6},{8,9},{9,8},{10,11... | collective-permute-start | bytes 1769480 | tf_op jit(solution)/shard_map/ppermute | solution.py:238
  202.7 27.6 %collective-permute-start.25 = (bf16[2,2,2,2,1,12,1536]{6,3,5,4,2,1,0:T(2,128)(2,1)}, bf16[2,2,2,2,1,12,1536]{6,3,5,4,2,1,0:T(2,128)(2,1)}, u32[]{:S(2)}, u32[]{:S(2)}) collective-permute-start(bf16[2,2,2,2,1,12,1536]{6,3,5,4,2,1,0:T(2,128)(2,1)} %copy.204), channel_id=1, source_target_pairs={{0,1},{1,0},{2,3},{3,2},{4,5},{5,4},{6,7},{7,6},{8,9},{9,8},{10,11... | collective-permute-start | bytes 1769480 | tf_op jit(solution)/shard_map/ppermute | solution.py:238
  218.1 9.9 %collective-permute-start.39 = (bf16[1,1,1,1,1,144]{5,4,3,2,1,0:T(2,128)(2,1)S(1)}, bf16[1,1,1,1,1,144]{5,4,3,2,1,0:T(2,128)(2,1)S(1)}, u32[]{:S(2)}, u32[]{:S(2)}) collective-permute-start(bf16[1,1,1,1,1,144]{5,4,3,2,1,0:T(2,128)(2,1)S(1)} %constant_dynamic-slice_fusion), channel_id=1, source_target_pairs={{0,4},{1,5},{2,6},{3,7},{4,0},{5,1},{6,2},{7,3},{8,12},{9,13},{10,... | collective-permute-start | bytes 872 | tf_op jit(solution)/shard_map/ppermute | solution.py:238
  220.6 11.7 %collective-permute-start.20 = (bf16[2,2,2,2,1,12,1536]{6,3,5,4,2,1,0:T(2,128)(2,1)S(1)}, bf16[2,2,2,2,1,12,1536]{6,3,5,4,2,1,0:T(2,128)(2,1)S(1)}, u32[]{:S(2)}, u32[]{:S(2)}) collective-permute-start(bf16[2,2,2,2,1,12,1536]{6,3,5,4,2,1,0:T(2,128)(2,1)S(1)} %copy.202), channel_id=1, source_target_pairs={{0,1},{1,0},{2,3},{3,2},{4,5},{5,4},{6,7},{7,6},{8,9},{9,8},{10,11... | collective-permute-start | bytes 1769480 | tf_op jit(solution)/shard_map/ppermute | solution.py:238
  230.0 11.6 %collective-permute-start.31 = (bf16[2,2,2,1,1,12,1536]{6,5,4,3,2,1,0:T(8,128)(2,1)S(1)}, bf16[2,2,2,1,1,12,1536]{6,5,4,3,2,1,0:T(8,128)(2,1)S(1)}, u32[]{:S(2)}, u32[]{:S(2)}) collective-permute-start(bf16[2,2,2,1,1,12,1536]{6,5,4,3,2,1,0:T(8,128)(2,1)S(1)} %constant_dynamic-slice_fusion.11), channel_id=1, source_target_pairs={{0,2},{1,3},{2,0},{3,1},{4,6},{5,7},{6,4},{7,5},{8,10},{9,11},{10,... | collective-permute-start | bytes 884744 | tf_op jit(solution)/shard_map/ppermute | solution.py:238
  231.7 11.3 %collective-permute-start.26 = (bf16[1,2,2,2,1,12,1536]{6,5,4,3,2,1,0:T(8,128)(2,1)S(1)}, bf16[1,2,2,2,1,12,1536]{6,5,4,3,2,1,0:T(8,128)(2,1)S(1)}, u32[]{:S(2)}, u32[]{:S(2)}) collective-permute-start(bf16[1,2,2,2,1,12,1536]{6,5,4,3,2,1,0:T(8,128)(2,1)S(1)} %constant_dynamic-slice_fusion.16), channel_id=1, source_target_pairs={{0,16},{1,17},{2,18},{3,19},{4,20},{5,21},{6,22},{7,23},{8,24},{9,... | collective-permute-start | bytes 884744 | tf_op jit(solution)/shard_map/ppermute | solution.py:238
  232.6 12.3 %collective-permute-start.21 = (bf16[2,1,2,2,1,12,1536]{6,5,4,3,2,1,0:T(8,128)(2,1)S(1)}, bf16[2,1,2,2,1,12,1536]{6,5,4,3,2,1,0:T(8,128)(2,1)S(1)}, u32[]{:S(2)}, u32[]{:S(2)}) collective-permute-start(bf16[2,1,2,2,1,12,1536]{6,5,4,3,2,1,0:T(8,128)(2,1)S(1)} %constant_dynamic-slice_fusion.21), channel_id=1, source_target_pairs={{0,8},{1,9},{2,10},{3,11},{4,12},{5,13},{6,14},{7,15},{8,0},{9,1},... | collective-permute-start | bytes 884744 | tf_op jit(solution)/shard_map/ppermute | solution.py:238
  241.7 11.6 %collective-permute-start.32 = (bf16[2,2,1,1,1,12,1536]{6,5,4,3,2,1,0:T(8,128)(2,1)S(1)}, bf16[2,2,1,1,1,12,1536]{6,5,4,3,2,1,0:T(8,128)(2,1)S(1)}, u32[]{:S(2)}, u32[]{:S(2)}) collective-permute-start(bf16[2,2,1,1,1,12,1536]{6,5,4,3,2,1,0:T(8,128)(2,1)S(1)} %constant_dynamic-slice_fusion.10), channel_id=1, source_target_pairs={{0,4},{1,5},{2,6},{3,7},{4,0},{5,1},{6,2},{7,3},{8,12},{9,13},{10,... | collective-permute-start | bytes 442376 | tf_op jit(solution)/shard_map/ppermute | solution.py:238
  243.2 11.7 %collective-permute-start.27 = (bf16[1,2,2,1,1,12,1536]{6,5,4,3,2,1,0:T(8,128)(2,1)S(1)}, bf16[1,2,2,1,1,12,1536]{6,5,4,3,2,1,0:T(8,128)(2,1)S(1)}, u32[]{:S(2)}, u32[]{:S(2)}) collective-permute-start(bf16[1,2,2,1,1,12,1536]{6,5,4,3,2,1,0:T(8,128)(2,1)S(1)} %constant_dynamic-slice_fusion.15), channel_id=1, source_target_pairs={{0,2},{1,3},{2,0},{3,1},{4,6},{5,7},{6,4},{7,5},{8,10},{9,11},{10,... | collective-permute-start | bytes 442376 | tf_op jit(solution)/shard_map/ppermute | solution.py:238
  245.0 10.1 %collective-permute-start.22 = (bf16[1,1,2,2,1,12,1536]{6,5,4,3,2,1,0:T(8,128)(2,1)S(1)}, bf16[1,1,2,2,1,12,1536]{6,5,4,3,2,1,0:T(8,128)(2,1)S(1)}, u32[]{:S(2)}, u32[]{:S(2)}) collective-permute-start(bf16[1,1,2,2,1,12,1536]{6,5,4,3,2,1,0:T(8,128)(2,1)S(1)} %constant_dynamic-slice_fusion.20), channel_id=1, source_target_pairs={{0,16},{1,17},{2,18},{3,19},{4,20},{5,21},{6,22},{7,23},{8,24},{9,... | collective-permute-start | bytes 442376 | tf_op jit(solution)/shard_map/ppermute | solution.py:238
  (22 other events, 101.3 us)

commit v2 on v1

--- a/solution.py
+++ b/solution.py
@@ -16,6 +16,8 @@
 GROUP = 2
 CHUNK = 384
 PAIR = 2 * HD
+BLOCKS = 32
+ROWS = D // BLOCKS
 F32 = jnp.float32
 BF16 = jnp.bfloat16
 
@@ -46,9 +48,9 @@
 
 
 def kernel(
-    length, padded, counts, x_ref, ct_ref, wqkv, wout, wup, wdown, vec,
-    block_out, input_grad, gqkv, gout, gup, gdown, gvec,
-    aqkv, aout, aup, adown, avec, xs, es, qkv_s, mix_s, dmix_s, dqkv_s, p_s,
+    length, padded, counts, x_ref, ct_ref, wfirst, wup_in, wdown, vec,
+    block_out, input_grad, gfirst, gup, gdown, gvec,
+    wqkv, wout, wup, aqkv, aout, aup, adown, avec, xs, es, qkv_s, mix_s, dmix_s, dqkv_s, p_s,
 ):
     step = pl.program_id(0)
 
@@ -56,6 +58,16 @@
     def _():
         for ref in (aqkv, aout, aup, adown, avec, xs, es):
             ref[...] = jnp.zeros_like(ref)
+        for at in range(0, BLOCKS, 4):
+            rows = slice(at * ROWS, (at + 4) * ROWS)
+            for ref, outs in ((wfirst, (wqkv, wout)), (wup_in, (wup,))):
+                joined = jnp.concatenate([ref[at + k].astype(F32) for k in range(4)], axis=0)
+                joined = joined.astype(BF16)
+                if len(outs) == 1:
+                    wup[rows, :] = joined
+                else:
+                    wqkv[rows, :] = joined[:, : 3 * D]
+                    wout[rows, :] = joined[:, 3 * D :]
 
     count = counts[0]
     for i in range(GROUP):
@@ -174,9 +186,14 @@
 
     @pl.when(step == pl.num_programs(0) - 1)
     def _():
-        gqkv[...] = aqkv[...].astype(BF16)
-        gout[...] = aout[...].astype(BF16)
-        gup[...] = aup[...].astype(BF16)
+        for at in range(0, BLOCKS, 4):
+            rows = slice(at * ROWS, (at + 4) * ROWS)
+            first = jnp.concatenate([aqkv[rows, :], aout[rows, :]], axis=1)
+            up = aup[rows, :]
+            for k in range(4):
+                own = slice(k * ROWS, (k + 1) * ROWS)
+                gfirst[at + k] = first[own].astype(BF16)
+                gup[at + k] = up[own].astype(BF16)
         gdown[...] = adown[...].T.astype(BF16)
         gvec[...] = avec[...]
 
@@ -188,9 +205,9 @@
     image_spec = pl.BlockSpec((GROUP, length, D), lambda s: (s, 0, 0))
 
     def whole(shape):
-        return pl.BlockSpec(shape, lambda s: (0, 0))
-
-    shapes = [(D, 3 * D), (D, D), (D, FF), (FF, D)]
+        return pl.BlockSpec(shape, lambda s: (0,) * len(shape))
+
+    shapes = [(BLOCKS, ROWS, 4 * D), (BLOCKS, ROWS, FF), (FF, D)]
     vec_shape = (1, 8 * D + FF)
     flops = 3 * 2 * slots * length * (3 * D * D + D * D + 2 * D * FF)
     return pl.pallas_call(
@@ -207,6 +224,9 @@
         + [jax.ShapeDtypeStruct(s, BF16) for s in shapes]
         + [jax.ShapeDtypeStruct(vec_shape, F32)],
         scratch_shapes=[
+            pltpu.VMEM((D, 3 * D), BF16),
+            pltpu.VMEM((D, D), BF16),
+            pltpu.VMEM((D, FF), BF16),
             pltpu.VMEM((D, 3 * D), F32),
             pltpu.VMEM((D, D), F32),
             pltpu.VMEM((D, FF), F32),
@@ -274,31 +294,34 @@
         me = lax.axis_index(AXES)
 
         def shard(flat, width):
-            return flat if rows_each is None else flat.reshape(rows_each, width)
+            return flat if rows_each is None else flat.reshape(-1, width)
 
         first = jnp.concatenate([shard(qkv_flat, 3 * D), shard(out_flat, D)], axis=-1)
-        parts = [first, shard(up_flat, FF), shard(down_flat, FF)]
+        parts = [first, shard(up_flat, FF), shard(down_flat, D)]
         first, up, down = [gather(v, o, bits, me) for v, o in zip(parts, orders)]
         vec = gather(vectors, orders[0], bits, me)
         cut = qkv_flat.shape[0] if rows_each is None else 3 * D
+        if rows_each is None:
+            pair = [first[:, :cut].reshape(D, 3 * D), first[:, cut:].reshape(D, D)]
+            first = jnp.concatenate(pair, axis=1)
         weights = [
-            first[..., :cut].reshape(D, 3 * D),
-            first[..., cut:].reshape(D, D),
-            up.reshape(D, FF),
+            first.reshape(BLOCKS, ROWS, 4 * D),
+            up.reshape(BLOCKS, ROWS, FF),
             down.reshape(FF, D),
         ]
         vec = vec.astype(F32).reshape(1, -1)
-        block_out, input_grad, gqkv, gout, gup, gdown, gvec = block(
+        block_out, input_grad, gfirst, gup, gdown, gvec = block(
             images, counts, weights, vec, cotangent
         )
-
-        def blocks(grad, width):
-            if rows_each is None:
-                return grad.reshape(devices, -1)
-            return grad.reshape(devices, rows_each, width)
-
-        gfirst = jnp.concatenate([blocks(gqkv, 3 * D), blocks(gout, D)], axis=-1)
-        grads = [gfirst, blocks(gup, FF), blocks(gdown, FF)]
+        if rows_each is None:
+            both = gfirst.reshape(D, 4 * D)
+            pair = [both[:, : 3 * D], both[:, 3 * D :]]
+            gfirst = jnp.concatenate([g.reshape(devices, -1) for g in pair], axis=1)
+            gup, gdown = [g.reshape(devices, -1) for g in (gup, gdown)]
+        else:
+            gfirst, gup = [g.reshape(devices, rows_each, 4 * D) for g in (gfirst, gup)]
+            gdown = gdown.reshape(devices, -1, D)
+        grads = [gfirst, gup, gdown]
         gfirst, gup, gdown = [reduce_scatter(g, o, bits, me) for g, o in zip(grads, orders)]
         gvec = reduce_scatter(gvec.reshape(devices, -1), orders[0], bits, me)
         return (

time: 271 us -> 244 us (0.900)
  local copies, waits for them, and re-layouts: 57.7 us -> 32.3 us
  waiting for transfers between devices: 56.4 us -> 52.1 us
    select_n x9 -> x5, local copies, waits for them, and re-layouts: 12.5 us -> 5.47 us  [gather(): jnp.where(upper == 1, jnp.concatenate([other, held], axis=axis), jnp.conc...]
    unnamed x14 -> x18, local copies, waits for them, and re-layouts: 16.6 us -> 11.9 us
    another operation x3 -> x1, local copies, waits for them, and re-layouts: 4.66 us -> 0.11 us  [reduce_scatter(): held = value.reshape((2,) * bits + value.shape[1:])]
    ppermute x40, waiting for transfers between devices: 56.4 us -> 52.1 us  [swap(): lax.ppermute(value, AXES, [(d, d ^ 1 << bit) for d in range(devices)])]
    concatenate x3 -> x0, local copies, waits for them, and re-layouts: 4.03 us -> none  [body(): gfirst = jnp.concatenate([blocks(gqkv, 3 * D), blocks(gout, D)], axis=-1)]
    dynamic_slice x22 -> x17, local copies, waits for them, and re-layouts: 5.68 us -> 2.61 us  [reduce_scatter(): sent = lax.dynamic_index_in_dim(held, 1 - upper, axis, keepdims=True)]
  transfers between devices with their start and end apart: 40 -> 40, of which waited for: 15 -> 17; matrix products, arithmetic and copies ran while one was open for 21% -> 16% of each run, Pallas kernels for 0% -> 0%
where the time goes in v2:
time: 244 us
  Pallas kernels  109 us (45%)
  waiting for transfers between devices  52.1 us (21%)
  starting transfers between devices  39.1 us (16%)
  local copies, waits for them, and re-layouts  32.3 us (13%)
  other arithmetic  9.47 us (4%)
    pallas_call x1, Pallas kernels, block(): pl.pallas_call(functools.partial(kernel, length, padded), grid=(slots //...  109 us
    ppermute x40, waiting for transfers between devices, swap(): lax.ppermute(value, AXES, [(d, d ^ 1 << bit) for d in range(devices)])  52.1 us
    ppermute x40, starting transfers between devices, swap(): lax.ppermute(value, AXES, [(d, d ^ 1 << bit) for d in range(devices)])  39.1 us
    unnamed x18, local copies, waits for them, and re-layouts  11.9 us
    select_n x5, local copies, waits for them, and re-layouts, gather(): jnp.where(upper == 1, jnp.concatenate([other, held], axis=axis), jnp.conc...  5.47 us
  transfers between devices with their start and end apart: 40, of which 17 were waited for; matrix products, arithmetic and copies ran while one was open for 16% of the time, Pallas kernels for 0%

profile of v2, /device:TPU:0, one launch (start us, length us, event | category | flops | bytes accessed | tf_op | source)
XLA Modules:
  0.0 243.5 jit_solution(8168845581775866300)
XLA Ops:
  1.5 3.0 %collective-permute-start.5 = (bf16[1,1,1,1,1,12,1536]{6,5,4,3,2,1,0:T(8,128)(2,1)S(1)}, bf16[1,1,1,1,1,12,1536]{6,5,4,3,2,1,0:T(8,128)(2,1)S(1)}, u32[]{:S(2)}, u32[]{:S(2)}) collective-permute-start(bf16[1,1,1,1,1,12,1536]{6,5,4,3,2,1,0:T(8,128)(2,1)S(1)} %reshape_reshape.19), channel_id=1, source_target_pairs={{0,8},{1,9},{2,10},{3,11},{4,12},{5,13},{6,14},{7,15},{8,0},{9,1},... | collective-permute-start | bytes 110600 | tf_op jit(solution)/shard_map/ppermute | solution.py:258
  8.4 2.7 %collective-permute-start = (bf16[1,1,1,1,1,12,1536]{6,5,2,3,0,4,1:T(8,128)(2,1)S(1)}, bf16[1,1,1,1,1,12,1536]{6,5,2,3,0,4,1:T(8,128)(2,1)S(1)}, u32[]{:S(2)}, u32[]{:S(2)}) collective-permute-start(bf16[1,1,1,1,1,12,1536]{6,5,2,3,0,4,1:T(8,128)(2,1)S(1)} %bitcast.111), channel_id=1, source_target_pairs={{0,4},{1,5},{2,6},{3,7},{4,0},{5,1},{6,2},{7,3},{8,12},{9,13},{10,... | collective-permute-start | bytes 110600 | tf_op jit(solution)/shard_map/ppermute | solution.py:258
  14.4 3.8 %copy.180.x_ref = bf16[16,197,384]{2,1,0:T(8,128)(2,1)} copy(bf16[16,197,384]{2,0,1:T(8,128)(2,1)} %param.8) | data formatting | bytes 4841472 | tf_op args[0]
  18.2 2.0 copy.181.ct_ref
  22.5 2.0 collective-permute-done.16
  25.1 3.0 %collective-permute-done.17 = bf16[1,1,2,2,1,144]{5,2,3,4,1,0:T(2,128)(2,1)S(1)} collective-permute-done((bf16[1,1,2,2,1,144]{5,2,3,4,1,0:T(2,128)(2,1)S(1)}, bf16[1,1,2,2,1,144]{5,2,3,4,1,0:T(2,128)(2,1)S(1)}, u32[]{:S(2)}, u32[]{:S(2)}) %collective-permute-start.17) | collective-permute-done | bytes 1184 | tf_op jit(solution)/shard_map/ppermute | solution.py:258
  28.8 3.1 %collective-permute-done.18 = bf16[2,1,2,2,1,144]{5,2,3,4,1,0:T(2,128)(2,1)S(1)} collective-permute-done((bf16[2,1,2,2,1,144]{5,2,3,4,1,0:T(2,128)(2,1)S(1)}, bf16[2,1,2,2,1,144]{5,2,3,4,1,0:T(2,128)(2,1)S(1)}, u32[]{:S(2)}, u32[]{:S(2)}) %collective-permute-start.18) | collective-permute-done | bytes 2336 | tf_op jit(solution)/shard_map/ppermute | solution.py:258
  32.0 2.7 %collective-permute-start.6 = (bf16[1,2,1,1,1,12,1536]{6,5,2,3,0,4,1:T(8,128)(2,1)S(1)}, bf16[1,2,1,1,1,12,1536]{6,5,2,3,0,4,1:T(8,128)(2,1)S(1)}, u32[]{:S(2)}, u32[]{:S(2)}) collective-permute-start(bf16[1,2,1,1,1,12,1536]{6,5,2,3,0,4,1:T(8,128)(2,1)S(1)} %fusion.3), channel_id=1, source_target_pairs={{0,4},{1,5},{2,6},{3,7},{4,0},{5,1},{6,2},{7,3},{8,12},{9,13},{10,... | collective-permute-start | bytes 221192 | tf_op jit(solution)/shard_map/ppermute | solution.py:258
  37.0 3.3 %collective-permute-done.6 = bf16[1,2,1,1,1,12,1536]{6,5,2,3,0,4,1:T(8,128)(2,1)S(1)} collective-permute-done((bf16[1,2,1,1,1,12,1536]{6,5,2,3,0,4,1:T(8,128)(2,1)S(1)}, bf16[1,2,1,1,1,12,1536]{6,5,2,3,0,4,1:T(8,128)(2,1)S(1)}, u32[]{:S(2)}, u32[]{:S(2)}) %collective-permute-start.6) | collective-permute-done | bytes 73760 | tf_op jit(solution)/shard_map/ppermute | solution.py:258
  41.3 3.4 %collective-permute-start.12 = (bf16[2,2,1,1,1,48,384]{6,5,1,0,4,3,2:T(8,128)(2,1)S(1)}, bf16[2,2,1,1,1,48,384]{6,5,1,0,4,3,2:T(8,128)(2,1)S(1)}, u32[]{:S(2)}, u32[]{:S(2)}) collective-permute-start(bf16[2,2,1,1,1,48,384]{6,5,1,0,4,3,2:T(8,128)(2,1)S(1)} %maximum_select_fusion.16), channel_id=1, source_target_pairs={{0,4},{1,5},{2,6},{3,7},{4,0},{5,1},{6,2},{7,3},{8,12},{9,13},{10,... | collective-permute-start | bytes 442376 | tf_op jit(solution)/shard_map/ppermute | solution.py:258
  45.5 4.8 %collective-permute-done.7 = bf16[1,2,2,1,1,12,1536]{6,5,2,3,0,4,1:T(8,128)(2,1)S(1)} collective-permute-done((bf16[1,2,2,1,1,12,1536]{6,5,2,3,0,4,1:T(8,128)(2,1)S(1)}, bf16[1,2,2,1,1,12,1536]{6,5,2,3,0,4,1:T(8,128)(2,1)S(1)}, u32[]{:S(2)}, u32[]{:S(2)}) %collective-permute-start.7) | collective-permute-done | bytes 147488 | tf_op jit(solution)/shard_map/ppermute | solution.py:258
  51.0 2.1 collective-permute-start.13
  54.0 6.1 %collective-permute-done.8 = bf16[1,2,2,2,1,12,1536]{6,5,2,3,0,4,1:T(8,128)(2,1)S(1)} collective-permute-done((bf16[1,2,2,2,1,12,1536]{6,5,2,3,0,4,1:T(8,128)(2,1)S(1)}, bf16[1,2,2,2,1,12,1536]{6,5,2,3,0,4,1:T(8,128)(2,1)S(1)}, u32[]{:S(2)}, u32[]{:S(2)}) %collective-permute-start.8) | collective-permute-done | bytes 294944 | tf_op jit(solution)/shard_map/ppermute | solution.py:258
  72.5 108.6 %shard_map.135 = (bf16[16,197,384]{2,1,0:T(8,128)(2,1)}, f32[16,197,384]{2,1,0:T(8,128)}, bf16[32,12,1536]{2,1,0:T(8,128)(2,1)}, bf16[32,12,1536]{2,1,0:T(8,128)...) custom-call(s32[1]{0:T(128)S(6)} %copy.230.counts, bf16[16,197,384]{2,1,0:T(8,128)(2,1)} %copy.180.x_ref, ...), custom_call_target="tpu_custom_call" | custom-call | flops 33464254464 | bytes 20971520 | tf_op jit(solution)/shard_map/pallas_call | solution.py:213
  183.9 3.1 %collective-permute-done.36 = bf16[2,1,2,2,1,144]{5,4,3,2,1,0:T(2,128)(2,1)S(1)} collective-permute-done((bf16[2,1,2,2,1,144]{5,4,3,2,1,0:T(2,128)(2,1)S(1)}, bf16[2,1,2,2,1,144]{5,4,3,2,1,0:T(2,128)(2,1)S(1)}, u32[]{:S(2)}, u32[]{:S(2)}) %collective-permute-start.36) | collective-permute-done | bytes 2336 | tf_op jit(solution)/shard_map/ppermute | solution.py:258
  191.1 2.3 constant_dynamic-slice_fusion.18
  194.8 2.1 collective-permute-start.39
  197.1 3.1 %copy.187 = f32[16,197,384]{2,0,1:T(8,128)} copy(f32[16,197,384]{2,1,0:T(8,128)S(1)} %bitcast.88) | data formatting | bytes 9682944
  207.6 4.5 %collective-permute-done.31 = bf16[2,2,2,1,1,48,384]{6,5,4,3,2,1,0:T(8,128)(2,1)S(1)} collective-permute-done((bf16[2,2,2,1,1,48,384]{6,5,4,3,2,1,0:T(8,128)(2,1)S(1)}, bf16[2,2,2,1,1,48,384]{6,5,4,3,2,1,0:T(8,128)(2,1)S(1)}, u32[]{:S(2)}, u32[]{:S(2)}) %collective-permute-start.31) | collective-permute-done | bytes 294944 | tf_op jit(solution)/shard_map/ppermute | solution.py:258
  217.3 4.3 %collective-permute-done.32 = bf16[2,2,1,1,1,48,384]{6,5,4,3,2,1,0:T(8,128)(2,1)S(1)} collective-permute-done((bf16[2,2,1,1,1,48,384]{6,5,4,3,2,1,0:T(8,128)(2,1)S(1)}, bf16[2,2,1,1,1,48,384]{6,5,4,3,2,1,0:T(8,128)(2,1)S(1)}, u32[]{:S(2)}, u32[]{:S(2)}) %collective-permute-start.32) | collective-permute-done | bytes 147488 | tf_op jit(solution)/shard_map/ppermute | solution.py:258
  222.3 3.0 %collective-permute-done.27 = bf16[1,2,2,1,1,12,1536]{6,3,5,4,2,1,0:T(2,128)(2,1)S(1)} collective-permute-done((bf16[1,2,2,1,1,12,1536]{6,3,5,4,2,1,0:T(2,128)(2,1)S(1)}, bf16[1,2,2,1,1,12,1536]{6,3,5,4,2,1,0:T(2,128)(2,1)S(1)}, u32[]{:S(2)}, u32[]{:S(2)}) %collective-permute-start.27) | collective-permute-done | bytes 147488 | tf_op jit(solution)/shard_map/ppermute | solution.py:258
  226.9 2.4 collective-permute-start.23
  230.3 4.5 %collective-permute-done.23 = bf16[1,1,2,1,1,12,1536]{6,3,5,4,2,1,0:T(2,128)(2,1)S(1)} collective-permute-done((bf16[1,1,2,1,1,12,1536]{6,3,5,4,2,1,0:T(2,128)(2,1)S(1)}, bf16[1,1,2,1,1,12,1536]{6,3,5,4,2,1,0:T(2,128)(2,1)S(1)}, u32[]{:S(2)}, u32[]{:S(2)}) %collective-permute-start.23) | collective-permute-done | bytes 73760 | tf_op jit(solution)/shard_map/ppermute | solution.py:258
  236.2 4.6 %collective-permute-done.24 = bf16[1,1,1,1,1,12,1536]{6,3,5,4,2,1,0:T(2,128)(2,1)S(1)} collective-permute-done((bf16[1,1,1,1,1,12,1536]{6,3,5,4,2,1,0:T(2,128)(2,1)S(1)}, bf16[1,1,1,1,1,12,1536]{6,3,5,4,2,1,0:T(2,128)(2,1)S(1)}, u32[]{:S(2)}, u32[]{:S(2)}) %collective-permute-start.24) | collective-permute-done | bytes 36896 | tf_op jit(solution)/shard_map/ppermute | solution.py:258
  (177 shorter events, 57.4 us)
Async XLA Ops:
  1.5 30.4 %collective-permute-start.5 = (bf16[1,1,1,1,1,12,1536]{6,5,4,3,2,1,0:T(8,128)(2,1)S(1)}, bf16[1,1,1,1,1,12,1536]{6,5,4,3,2,1,0:T(8,128)(2,1)S(1)}, u32[]{:S(2)}, u32[]{:S(2)}) collective-permute-start(bf16[1,1,1,1,1,12,1536]{6,5,4,3,2,1,0:T(8,128)(2,1)S(1)} %reshape_reshape.19), channel_id=1, source_target_pairs={{0,8},{1,9},{2,10},{3,11},{4,12},{5,13},{6,14},{7,15},{8,0},{9,1},... | collective-permute-start | bytes 110600 | tf_op jit(solution)/shard_map/ppermute | solution.py:258
  5.3 29.3 %collective-permute-start.10 = (bf16[1,1,1,1,1,48,384]{6,5,4,3,2,1,0:T(8,128)(2,1)S(1)}, bf16[1,1,1,1,1,48,384]{6,5,4,3,2,1,0:T(8,128)(2,1)S(1)}, u32[]{:S(2)}, u32[]{:S(2)}) collective-permute-start(bf16[1,1,1,1,1,48,384]{6,5,4,3,2,1,0:T(8,128)(2,1)S(1)} %reshape_reshape.20), channel_id=1, source_target_pairs={{0,16},{1,17},{2,18},{3,19},{4,20},{5,21},{6,22},{7,23},{8,24},{9,... | collective-permute-start | bytes 110600 | tf_op jit(solution)/shard_map/ppermute | solution.py:258
  8.4 26.8 %collective-permute-start = (bf16[1,1,1,1,1,12,1536]{6,5,2,3,0,4,1:T(8,128)(2,1)S(1)}, bf16[1,1,1,1,1,12,1536]{6,5,2,3,0,4,1:T(8,128)(2,1)S(1)}, u32[]{:S(2)}, u32[]{:S(2)}) collective-permute-start(bf16[1,1,1,1,1,12,1536]{6,5,2,3,0,4,1:T(8,128)(2,1)S(1)} %bitcast.111), channel_id=1, source_target_pairs={{0,4},{1,5},{2,6},{3,7},{4,0},{5,1},{6,2},{7,3},{8,12},{9,13},{10,... | collective-permute-start | bytes 110600 | tf_op jit(solution)/shard_map/ppermute | solution.py:258
  11.7 9.1 %collective-permute-start.15 = (bf16[1,1,1,1,1,144]{5,2,3,4,1,0:T(2,128)(2,1)S(1)}, bf16[1,1,1,1,1,144]{5,2,3,4,1,0:T(2,128)(2,1)S(1)}, u32[]{:S(2)}, u32[]{:S(2)}) collective-permute-start(bf16[1,1,1,1,1,144]{5,2,3,4,1,0:T(2,128)(2,1)S(1)} %reshape.2885), channel_id=1, source_target_pairs={{0,4},{1,5},{2,6},{3,7},{4,0},{5,1},{6,2},{7,3},{8,12},{9,13},{10,... | collective-permute-start | bytes 872 | tf_op jit(solution)/shard_map/ppermute | solution.py:258
  31.8 34.0 %collective-permute-start.19 = (bf16[2,2,2,2,1,144]{5,2,3,4,1,0:T(2,128)(2,1)S(1)}, bf16[2,2,2,2,1,144]{5,2,3,4,1,0:T(2,128)(2,1)S(1)}, u32[]{:S(2)}, u32[]{:S(2)}) collective-permute-start(bf16[2,2,2,2,1,144]{5,2,3,4,1,0:T(2,128)(2,1)S(1)} %broadcast_select_fusion.1), channel_id=1, source_target_pairs={{0,1},{1,0},{2,3},{3,2},{4,5},{5,4},{6,7},{7,6},{8,9},{9,8},{10,11... | collective-permute-start | bytes 13832 | tf_op jit(solution)/shard_map/ppermute | solution.py:258
  32.0 8.4 %collective-permute-start.6 = (bf16[1,2,1,1,1,12,1536]{6,5,2,3,0,4,1:T(8,128)(2,1)S(1)}, bf16[1,2,1,1,1,12,1536]{6,5,2,3,0,4,1:T(8,128)(2,1)S(1)}, u32[]{:S(2)}, u32[]{:S(2)}) collective-permute-start(bf16[1,2,1,1,1,12,1536]{6,5,2,3,0,4,1:T(8,128)(2,1)S(1)} %fusion.3), channel_id=1, source_target_pairs={{0,4},{1,5},{2,6},{3,7},{4,0},{5,1},{6,2},{7,3},{8,12},{9,13},{10,... | collective-permute-start | bytes 221192 | tf_op jit(solution)/shard_map/ppermute | solution.py:258
  35.3 9.4 %collective-permute-start.1 = (bf16[1,1,2,1,1,12,1536]{6,5,2,3,0,4,1:T(8,128)(2,1)S(1)}, bf16[1,1,2,1,1,12,1536]{6,5,2,3,0,4,1:T(8,128)(2,1)S(1)}, u32[]{:S(2)}, u32[]{:S(2)}) collective-permute-start(bf16[1,1,2,1,1,12,1536]{6,5,2,3,0,4,1:T(8,128)(2,1)S(1)} %maximum_select_fusion.17), channel_id=1, source_target_pairs={{0,2},{1,3},{2,0},{3,1},{4,6},{5,7},{6,4},{7,5},{8,10},{9,11},{10,... | collective-permute-start | bytes 221192 | tf_op jit(solution)/shard_map/ppermute | solution.py:258
  40.6 9.6 %collective-permute-start.7 = (bf16[1,2,2,1,1,12,1536]{6,5,2,3,0,4,1:T(8,128)(2,1)S(1)}, bf16[1,2,2,1,1,12,1536]{6,5,2,3,0,4,1:T(8,128)(2,1)S(1)}, u32[]{:S(2)}, u32[]{:S(2)}) collective-permute-start(bf16[1,2,2,1,1,12,1536]{6,5,2,3,0,4,1:T(8,128)(2,1)S(1)} %maximum_select_fusion.14), channel_id=1, source_target_pairs={{0,2},{1,3},{2,0},{3,1},{4,6},{5,7},{6,4},{7,5},{8,10},{9,11},{10,... | collective-permute-start | bytes 442376 | tf_op jit(solution)/shard_map/ppermute | solution.py:258
  41.3 9.6 %collective-permute-start.12 = (bf16[2,2,1,1,1,48,384]{6,5,1,0,4,3,2:T(8,128)(2,1)S(1)}, bf16[2,2,1,1,1,48,384]{6,5,1,0,4,3,2:T(8,128)(2,1)S(1)}, u32[]{:S(2)}, u32[]{:S(2)}) collective-permute-start(bf16[2,2,1,1,1,48,384]{6,5,1,0,4,3,2:T(8,128)(2,1)S(1)} %maximum_select_fusion.16), channel_id=1, source_target_pairs={{0,4},{1,5},{2,6},{3,7},{4,0},{5,1},{6,2},{7,3},{8,12},{9,13},{10,... | collective-permute-start | bytes 442376 | tf_op jit(solution)/shard_map/ppermute | solution.py:258
  44.8 8.3 %collective-permute-start.2 = (bf16[1,1,2,2,1,12,1536]{6,5,2,3,0,4,1:T(8,128)(2,1)S(1)}, bf16[1,1,2,2,1,12,1536]{6,5,2,3,0,4,1:T(8,128)(2,1)S(1)}, u32[]{:S(2)}, u32[]{:S(2)}) collective-permute-start(bf16[1,1,2,2,1,12,1536]{6,5,2,3,0,4,1:T(8,128)(2,1)S(1)} %maximum_select_fusion.12), channel_id=1, source_target_pairs={{0,16},{1,17},{2,18},{3,19},{4,20},{5,21},{6,22},{7,23},{8,24},{9,... | collective-permute-start | bytes 442376 | tf_op jit(solution)/shard_map/ppermute | solution.py:258
  50.3 9.8 %collective-permute-start.8 = (bf16[1,2,2,2,1,12,1536]{6,5,2,3,0,4,1:T(8,128)(2,1)S(1)}, bf16[1,2,2,2,1,12,1536]{6,5,2,3,0,4,1:T(8,128)(2,1)S(1)}, u32[]{:S(2)}, u32[]{:S(2)}) collective-permute-start(bf16[1,2,2,2,1,12,1536]{6,5,2,3,0,4,1:T(8,128)(2,1)S(1)} %maximum_select_fusion.8), channel_id=1, source_target_pairs={{0,16},{1,17},{2,18},{3,19},{4,20},{5,21},{6,22},{7,23},{8,24},{9,... | collective-permute-start | bytes 884744 | tf_op jit(solution)/shard_map/ppermute | solution.py:258
  51.0 14.2 %collective-permute-start.13 = (bf16[2,2,2,1,1,48,384]{6,5,4,3,2,1,0:T(8,128)(2,1)S(1)}, bf16[2,2,2,1,1,48,384]{6,5,4,3,2,1,0:T(8,128)(2,1)S(1)}, u32[]{:S(2)}, u32[]{:S(2)}) collective-permute-start(bf16[2,2,2,1,1,48,384]{6,5,4,3,2,1,0:T(8,128)(2,1)S(1)} %copy.175), channel_id=1, source_target_pairs={{0,2},{1,3},{2,0},{3,1},{4,6},{5,7},{6,4},{7,5},{8,10},{9,11},{10,... | collective-permute-start | bytes 884744 | tf_op jit(solution)/shard_map/ppermute | solution.py:258
  53.1 10.4 %collective-permute-start.3 = (bf16[2,1,2,2,1,12,1536]{6,5,2,3,0,4,1:T(8,128)(2,1)S(1)}, bf16[2,1,2,2,1,12,1536]{6,5,2,3,0,4,1:T(8,128)(2,1)S(1)}, u32[]{:S(2)}, u32[]{:S(2)}) collective-permute-start(bf16[2,1,2,2,1,12,1536]{6,5,2,3,0,4,1:T(8,128)(2,1)S(1)} %maximum_select_fusion.6), channel_id=1, source_target_pairs={{0,8},{1,9},{2,10},{3,11},{4,12},{5,13},{6,14},{7,15},{8,0},{9,1},... | collective-permute-start | bytes 884744 | tf_op jit(solution)/shard_map/ppermute | solution.py:258
  188.8 13.8 %collective-permute-start.30 = (bf16[2,2,2,2,1,48,384]{6,5,4,3,2,1,0:T(8,128)(2,1)S(1)}, bf16[2,2,2,2,1,48,384]{6,5,4,3,2,1,0:T(8,128)(2,1)S(1)}, u32[]{:S(2)}, u32[]{:S(2)}) collective-permute-start(bf16[2,2,2,2,1,48,384]{6,5,4,3,2,1,0:T(8,128)(2,1)S(1)} %constant_dynamic-slice_fusion.12), channel_id=1, source_target_pairs={{0,1},{1,0},{2,3},{3,2},{4,5},{5,4},{6,7},{7,6},{8,9},{9,8},{10,11... | collective-permute-start | bytes 1769480 | tf_op jit(solution)/shard_map/ppermute | solution.py:258
  194.0 9.9 %collective-permute-start.25 = (bf16[2,2,2,2,1,12,1536]{6,3,5,4,2,1,0:T(2,128)(2,1)S(1)}, bf16[2,2,2,2,1,12,1536]{6,3,5,4,2,1,0:T(2,128)(2,1)S(1)}, u32[]{:S(2)}, u32[]{:S(2)}) collective-permute-start(bf16[2,2,2,2,1,12,1536]{6,3,5,4,2,1,0:T(2,128)(2,1)S(1)} %copy.205), channel_id=1, source_target_pairs={{0,1},{1,0},{2,3},{3,2},{4,5},{5,4},{6,7},{7,6},{8,9},{9,8},{10,11... | collective-permute-start | bytes 1769480 | tf_op jit(solution)/shard_map/ppermute | solution.py:258
  196.9 9.1 %collective-permute-start.20 = (bf16[2,2,2,2,1,12,1536]{6,3,5,4,2,1,0:T(2,128)(2,1)S(1)}, bf16[2,2,2,2,1,12,1536]{6,3,5,4,2,1,0:T(2,128)(2,1)S(1)}, u32[]{:S(2)}, u32[]{:S(2)}) collective-permute-start(bf16[2,2,2,2,1,12,1536]{6,3,5,4,2,1,0:T(2,128)(2,1)S(1)} %copy.203), channel_id=1, source_target_pairs={{0,1},{1,0},{2,3},{3,2},{4,5},{5,4},{6,7},{7,6},{8,9},{9,8},{10,11... | collective-permute-start | bytes 1769480 | tf_op jit(solution)/shard_map/ppermute | solution.py:258
  202.8 9.3 %collective-permute-start.31 = (bf16[2,2,2,1,1,48,384]{6,5,4,3,2,1,0:T(8,128)(2,1)S(1)}, bf16[2,2,2,1,1,48,384]{6,5,4,3,2,1,0:T(8,128)(2,1)S(1)}, u32[]{:S(2)}, u32[]{:S(2)}) collective-permute-start(bf16[2,2,2,1,1,48,384]{6,5,4,3,2,1,0:T(8,128)(2,1)S(1)} %constant_dynamic-slice_fusion.11), channel_id=1, source_target_pairs={{0,2},{1,3},{2,0},{3,1},{4,6},{5,7},{6,4},{7,5},{8,10},{9,11},{10,... | collective-permute-start | bytes 884744 | tf_op jit(solution)/shard_map/ppermute | solution.py:258
  205.0 9.0 %collective-permute-start.26 = (bf16[1,2,2,2,1,12,1536]{6,3,5,4,2,1,0:T(2,128)(2,1)S(1)}, bf16[1,2,2,2,1,12,1536]{6,3,5,4,2,1,0:T(2,128)(2,1)S(1)}, u32[]{:S(2)}, u32[]{:S(2)}) collective-permute-start(bf16[1,2,2,2,1,12,1536]{6,3,5,4,2,1,0:T(2,128)(2,1)S(1)} %constant_dynamic-slice_fusion.16), channel_id=1, source_target_pairs={{0,16},{1,17},{2,18},{3,19},{4,20},{5,21},{6,22},{7,23},{8,24},{9,... | collective-permute-start | bytes 884744 | tf_op jit(solution)/shard_map/ppermute | solution.py:258
  207.0 8.7 %collective-permute-start.21 = (bf16[2,1,2,2,1,12,1536]{6,3,5,4,2,1,0:T(2,128)(2,1)S(1)}, bf16[2,1,2,2,1,12,1536]{6,3,5,4,2,1,0:T(2,128)(2,1)S(1)}, u32[]{:S(2)}, u32[]{:S(2)}) collective-permute-start(bf16[2,1,2,2,1,12,1536]{6,3,5,4,2,1,0:T(2,128)(2,1)S(1)} %constant_dynamic-slice_fusion.22), channel_id=1, source_target_pairs={{0,8},{1,9},{2,10},{3,11},{4,12},{5,13},{6,14},{7,15},{8,0},{9,1},... | collective-permute-start | bytes 884744 | tf_op jit(solution)/shard_map/ppermute | solution.py:258
  212.2 9.5 %collective-permute-start.32 = (bf16[2,2,1,1,1,48,384]{6,5,4,3,2,1,0:T(8,128)(2,1)S(1)}, bf16[2,2,1,1,1,48,384]{6,5,4,3,2,1,0:T(8,128)(2,1)S(1)}, u32[]{:S(2)}, u32[]{:S(2)}) collective-permute-start(bf16[2,2,1,1,1,48,384]{6,5,4,3,2,1,0:T(8,128)(2,1)S(1)} %constant_dynamic-slice_fusion.10), channel_id=1, source_target_pairs={{0,4},{1,5},{2,6},{3,7},{4,0},{5,1},{6,2},{7,3},{8,12},{9,13},{10,... | collective-permute-start | bytes 442376 | tf_op jit(solution)/shard_map/ppermute | solution.py:258
  214.6 10.7 %collective-permute-start.27 = (bf16[1,2,2,1,1,12,1536]{6,3,5,4,2,1,0:T(2,128)(2,1)S(1)}, bf16[1,2,2,1,1,12,1536]{6,3,5,4,2,1,0:T(2,128)(2,1)S(1)}, u32[]{:S(2)}, u32[]{:S(2)}) collective-permute-start(bf16[1,2,2,1,1,12,1536]{6,3,5,4,2,1,0:T(2,128)(2,1)S(1)} %constant_dynamic-slice_fusion.15), channel_id=1, source_target_pairs={{0,2},{1,3},{2,0},{3,1},{4,6},{5,7},{6,4},{7,5},{8,10},{9,11},{10,... | collective-permute-start | bytes 442376 | tf_op jit(solution)/shard_map/ppermute | solution.py:258
  216.2 10.4 %collective-permute-start.22 = (bf16[1,1,2,2,1,12,1536]{6,3,5,4,2,1,0:T(2,128)(2,1)S(1)}, bf16[1,1,2,2,1,12,1536]{6,3,5,4,2,1,0:T(2,128)(2,1)S(1)}, u32[]{:S(2)}, u32[]{:S(2)}) collective-permute-start(bf16[1,1,2,2,1,12,1536]{6,3,5,4,2,1,0:T(2,128)(2,1)S(1)} %constant_dynamic-slice_fusion.21), channel_id=1, source_target_pairs={{0,16},{1,17},{2,18},{3,19},{4,20},{5,21},{6,22},{7,23},{8,24},{9,... | collective-permute-start | bytes 442376 | tf_op jit(solution)/shard_map/ppermute | solution.py:258
  225.9 9.4 %collective-permute-start.28 = (bf16[1,2,1,1,1,12,1536]{6,3,5,4,2,1,0:T(2,128)(2,1)S(1)}, bf16[1,2,1,1,1,12,1536]{6,3,5,4,2,1,0:T(2,128)(2,1)S(1)}, u32[]{:S(2)}, u32[]{:S(2)}) collective-permute-start(bf16[1,2,1,1,1,12,1536]{6,3,5,4,2,1,0:T(2,128)(2,1)S(1)} %constant_dynamic-slice_fusion.14), channel_id=1, source_target_pairs={{0,4},{1,5},{2,6},{3,7},{4,0},{5,1},{6,2},{7,3},{8,12},{9,13},{10,... | collective-permute-start | bytes 221192 | tf_op jit(solution)/shard_map/ppermute | solution.py:258
  229.3 11.5 %collective-permute-start.34 = (bf16[1,1,1,1,1,48,384]{6,5,4,3,2,1,0:T(8,128)(2,1)S(1)}, bf16[1,1,1,1,1,48,384]{6,5,4,3,2,1,0:T(8,128)(2,1)S(1)}, u32[]{:S(2)}, u32[]{:S(2)}) collective-permute-start(bf16[1,1,1,1,1,48,384]{6,5,4,3,2,1,0:T(8,128)(2,1)S(1)} %constant_dynamic-slice_fusion.8), channel_id=1, source_target_pairs={{0,16},{1,17},{2,18},{3,19},{4,20},{5,21},{6,22},{7,23},{8,24},{9,... | collective-permute-start | bytes 110600 | tf_op jit(solution)/shard_map/ppermute | solution.py:258
  (21 other events, 101.0 us)
